TPU v7x, 768 devices: a whole 4x8x12 slice. The times are simulated.
768 devices in a mesh: vocab: 96 (over z, y), width: 8 (over x, core).
Axes of the slice: x: 4, y: 8, z: 12, core: 2. Of those that a mesh axis runs over, the one named last changes fastest.
Arguments:
- grad_out: bfloat16 [98304, 7168], P(('vocab', 'width')), may hold values from -6 to 6
- token_ids: int32 [98304], P('vocab'), may hold values from 0 to 18431, as said below
- slot_ids: int32 [96, 192], P('vocab'), may hold values from -1 to 18431, as said below
- param: float32 [18432, 7168], P('vocab', 'width'), may hold values from -6 to 6
- moment1: bfloat16 [18432, 7168], P('vocab', 'width'), may hold values from -4 to 4
- moment2: bfloat16 [18432, 7168], P('vocab', 'width'), may hold values from 0.0099487305 to 1
Outputs:
- new_param: float32 [18432, 7168], P('vocab', 'width')
- new_moment1: bfloat16 [18432, 7168], P('vocab', 'width')
- new_moment2: bfloat16 [18432, 7168], P('vocab', 'width')
Inputs may be any that keep to these rules, and one draw needn't show every extreme that they name: `token_ids`: every token's id is one of the ids that slot_ids lists in the row of the token's group. `slot_ids`: in row v, entries b * 2 to b * 2 + 1 list distinct ids of block b (ids b * 192 to (b + 1) * 192 - 1), used entries first, -1 for unused ones. In every draw some block has all 2 entries used in every row.
All inputs are finite; a program needn't handle non-finite values.
Results may differ from a plain program's by a relative error of at most 0.024.
Values may be sent and summed in bfloat16 or wider, within the bound.
No kernel may reach another device: no remote copies, remote signals or barrier semaphores. Data moves between devices by JAX's collectives and lax.ppermute only.
A program may use at most 32 MiB of HBM per device.

v0:
```python
import jax
import jax.numpy as jnp
from jax import lax
from jax.sharding import PartitionSpec as P

BETA_ONE = 0.9
BETA_TWO = 0.95
LEARN_RATE = 0.01
WEIGHT_DECAY = 0.1
EPSILON = 1e-08
CORRECT_ONE = 1.0 - 0.9**10
CORRECT_TWO = 1.0 - 0.95**10


def adamw_rows(param, moment1, moment2, table_grad):
    first_full = BETA_ONE * moment1.astype(jnp.float32) + (1.0 - BETA_ONE) * table_grad
    second_full = (
        BETA_TWO * moment2.astype(jnp.float32) + (1.0 - BETA_TWO) * table_grad * table_grad
    )
    new_moment1 = lax.optimization_barrier(first_full.astype(jnp.bfloat16))
    new_moment2 = lax.optimization_barrier(second_full.astype(jnp.bfloat16))
    first_round = new_moment1.astype(jnp.float32)
    second_round = new_moment2.astype(jnp.float32)
    update = first_round / CORRECT_ONE / (jnp.sqrt(second_round / CORRECT_TWO) + EPSILON)
    new_param = param - LEARN_RATE * (update + WEIGHT_DECAY * param)
    return (new_param, new_moment1, new_moment2)


def per_device(grad_out, token_ids, slot_ids, param, moment1, moment2):
    slot_list = slot_ids.reshape(-1)
    regrouped = lax.all_to_all(grad_out, "width", split_axis=1, concat_axis=0, tiled=True)
    onehot = (slot_list[:, None] == token_ids[None, :]).astype(jnp.bfloat16)
    summed = jnp.dot(onehot, regrouped, preferred_element_type=jnp.float32)
    outgoing = summed.astype(jnp.bfloat16)
    block_rows = param.shape[0]
    owner_index = lax.axis_index("vocab")
    arrived, arrived_ids = (
        lax.all_to_all(outgoing, "vocab", split_axis=0, concat_axis=0, tiled=True),
        lax.all_to_all(slot_list, "vocab", split_axis=0, concat_axis=0, tiled=True),
    )
    local_rows = arrived_ids - owner_index * block_rows
    selector = (lax.iota(jnp.int32, block_rows)[:, None] == local_rows[None, :]).astype(
        jnp.bfloat16
    )
    table_grad = jnp.dot(selector, arrived, preferred_element_type=jnp.float32)
    return adamw_rows(param, moment1, moment2, table_grad)


def solution(mesh):
    return jax.shard_map(
        per_device,
        mesh=mesh,
        in_specs=(
            P(("vocab", "width"), None),
            P("vocab"),
            P("vocab", None),
            P("vocab", "width"),
            P("vocab", "width"),
            P("vocab", "width"),
        ),
        out_specs=(P("vocab", "width"), P("vocab", "width"), P("vocab", "width")),
        check_vma=False,
    )
```

profile of v0, /device:TPU:6, one launch (start us, length us, event | category | flops | bytes accessed | tf_op | source)
XLA Modules:
  0.0 98.5 jit_solution(9644320769595553913)
XLA Ops:
  0.6 3.9 %copy.12 = bf16[128,7168]{0,1:T(8,128)(2,1)} copy(bf16[128,7168]{1,0:T(8,128)(2,1)} %param.6) | data formatting | bytes 3670016 | tf_op args[0]
  4.5 0.0 copy-start.3
  4.5 13.1 %all-to-all-start.1 = ((bf16[128,8,896]{0,2,1:T(8,128)(2,1)}), bf16[128,8,896]{0,2,1:T(8,128)(2,1)S(1)}, u32[]{:S(2)}, u32[]{:S(2)}) async-start(bf16[128,8,896]{0,2,1:T(8,128)(2,1)} %bitcast.8), calls=%async_computation.1 | async-start | bytes 3670016 | tf_op jit(solution)/shard_map/all_to_all | solution.py:31
  17.7 0.5 broadcast.21
  18.2 0.0 copy-done.3
  18.2 0.7 reduce.7
  18.8 0.8 all_to_all.28
  19.6 20.4 %all-to-all-done.1 = bf16[128,8,896]{0,2,1:T(8,128)(2,1)S(1)} async-done(((bf16[128,8,896]{0,2,1:T(8,128)(2,1)}), bf16[128,8,896]{0,2,1:T(8,128)(2,1)S(1)}, u32[]{:S(2)}, u32[]{:S(2)}) %all-to-all-start.1) | async-done | bytes 1835040 | tf_op jit(solution)/shard_map/all_to_all | solution.py:31
  40.0 13.8 %all-to-all-start = ((s32[96,2,1]{1,2,0:T(1,128)}), s32[96,2,1]{1,2,0:T(1,128)S(1)}, u32[]{:S(2)}, u32[]{:S(2)}) async-start(s32[96,2,1]{1,2,0:T(1,128)} %bitcast), calls=%async_computation | async-start | bytes 98304 | tf_op jit(solution)/shard_map/all_to_all | solution.py:39
  53.8 0.0 copy-start.6
  53.8 2.6 %copy.13 = bf16[8,128,896]{2,1,0:T(8,128)(2,1)} copy(bf16[8,128,896]{1,2,0:T(8,128)(2,1)S(1)} %bitcast.7) | data formatting | bytes 3670016 | tf_op jit(solution)/shard_map/all_to_all | solution.py:31
  56.4 0.0 copy-done.6
  56.4 0.0 copy-start.4
  56.4 0.0 copy-start.5
  56.4 2.2 %convolution_convert_fusion = bf16[192,896]{1,0:T(8,128)(2,1)S(1)} fusion(bf16[1024,896]{1,0:T(8,128)(2,1)} %bitcast.9, s32[1024]{0:T(1024)S(1)} %copy-done.6, s32[192]{0:T(256)S(1)} %bitcast.10), kind=kOutput, calls=%fused_computation | convolution fusion | flops 352690176 | bytes 2183936 | tf_op jit(solution)/shard_map/dot_general | solution.py:33
  58.6 0.9 all_to_all.34
  59.5 0.0 copy-start
  59.5 8.4 %all-to-all-done = s32[96,2,1]{1,2,0:T(1,128)S(1)} async-done(((s32[96,2,1]{1,2,0:T(1,128)}), s32[96,2,1]{1,2,0:T(1,128)S(1)}, u32[]{:S(2)}, u32[]{:S(2)}) %all-to-all-start) | async-done | bytes 800 | tf_op jit(solution)/shard_map/all_to_all | solution.py:39
  67.8 7.4 %all-to-all-start.2 = ((bf16[96,2,896]{2,1,0:T(2,128)(2,1)}), bf16[96,2,896]{2,1,0:T(2,128)(2,1)S(1)}, u32[]{:S(2)}, u32[]{:S(2)}) async-start(bf16[96,2,896]{2,1,0:T(2,128)(2,1)} %all_to_all.34), calls=%async_computation.2 | async-start | bytes 688128 | tf_op jit(solution)/shard_map/all_to_all | solution.py:38
  75.2 0.1 subtract_reduce_fusion
  75.4 0.1 sub.18
  75.5 21.2 %all-to-all-done.2 = bf16[96,2,896]{2,1,0:T(2,128)(2,1)S(1)} async-done(((bf16[96,2,896]{2,1,0:T(2,128)(2,1)}), bf16[96,2,896]{2,1,0:T(2,128)(2,1)S(1)}, u32[]{:S(2)}, u32[]{:S(2)}) %all-to-all-start.2) | async-done | bytes 344096 | tf_op jit(solution)/shard_map/all_to_all | solution.py:38
  96.7 0.1 all_to_all.36
  96.9 0.0 copy-done.4
  96.9 0.0 copy-done.5
  96.9 0.3 add_convert_fusion
  97.2 0.0 copy-start.1
  97.3 0.0 copy-start.2
  97.3 0.0 copy-done
  97.3 1.3 %multiply_subtract_fusion = f32[192,896]{1,0:T(8,128)} fusion(f32[192,896]{1,0:T(8,128)S(1)} %copy-done, bf16[192,896]{1,0:T(8,128)(2,1)S(1)} %get-tuple-element.4, bf16[192,896]{1,0:T(8,128)(2,1)S(1)} %get-tuple-element.3), kind=kLoop, calls=%fused_computation.5 | loop fusion | flops 1720320 | bytes 2064384 | tf_op jit(solution)/shard_map/sub | solution.py:25
  98.5 0.0 copy-done.1
  98.5 0.0 copy-done.2
Async XLA Ops:
  4.5 13.7 %copy-start.3 = (s32[1,192]{1,0:T(1,128)S(1)}, s32[1,192]{1,0:T(1,128)}, u32[]{:S(2)}) copy-start(s32[1,192]{1,0:T(1,128)} %param.8) | copy-start | bytes 2308
  4.5 35.4 %all-to-all-start.1 = ((bf16[128,8,896]{0,2,1:T(8,128)(2,1)}), bf16[128,8,896]{0,2,1:T(8,128)(2,1)S(1)}, u32[]{:S(2)}, u32[]{:S(2)}) async-start(bf16[128,8,896]{0,2,1:T(8,128)(2,1)} %bitcast.8), calls=%async_computation.1 | async-start | bytes 3670016 | tf_op jit(solution)/shard_map/all_to_all | solution.py:31
  40.0 27.9 %all-to-all-start = ((s32[96,2,1]{1,2,0:T(1,128)}), s32[96,2,1]{1,2,0:T(1,128)S(1)}, u32[]{:S(2)}, u32[]{:S(2)}) async-start(s32[96,2,1]{1,2,0:T(1,128)} %bitcast), calls=%async_computation | async-start | bytes 98304 | tf_op jit(solution)/shard_map/all_to_all | solution.py:39
  53.8 2.7 %copy-start.6 = (s32[1024]{0:T(1024)S(1)}, s32[1024]{0:T(1024)}, u32[]{:S(2)}) copy-start(s32[1024]{0:T(1024)} %param.7) | copy-start | bytes 12292
  56.4 40.5 %copy-start.4 = (bf16[192,896]{1,0:T(8,128)(2,1)S(1)}, bf16[192,896]{1,0:T(8,128)(2,1)}, u32[]{:S(2)}) copy-start(bf16[192,896]{1,0:T(8,128)(2,1)} %param.10) | copy-start | bytes 1032196
  56.4 40.5 %copy-start.5 = (bf16[192,896]{1,0:T(8,128)(2,1)S(1)}, bf16[192,896]{1,0:T(8,128)(2,1)}, u32[]{:S(2)}) copy-start(bf16[192,896]{1,0:T(8,128)(2,1)} %param.11) | copy-start | bytes 1032196
  59.5 37.8 %copy-start = (f32[192,896]{1,0:T(8,128)S(1)}, f32[192,896]{1,0:T(8,128)}, u32[]{:S(2)}) copy-start(f32[192,896]{1,0:T(8,128)} %param.9) | copy-start | bytes 2064388
  67.8 28.9 %all-to-all-start.2 = ((bf16[96,2,896]{2,1,0:T(2,128)(2,1)}), bf16[96,2,896]{2,1,0:T(2,128)(2,1)S(1)}, u32[]{:S(2)}, u32[]{:S(2)}) async-start(bf16[96,2,896]{2,1,0:T(2,128)(2,1)} %all_to_all.34), calls=%async_computation.2 | async-start | bytes 688128 | tf_op jit(solution)/shard_map/all_to_all | solution.py:38
  97.2 1.3 %copy-start.1 = (bf16[192,896]{1,0:T(8,128)(2,1)}, bf16[192,896]{1,0:T(8,128)(2,1)S(1)}, u32[]{:S(2)}) copy-start(bf16[192,896]{1,0:T(8,128)(2,1)S(1)} %get-tuple-element.3) | copy-start | bytes 1032196
  97.3 1.3 %copy-start.2 = (bf16[192,896]{1,0:T(8,128)(2,1)}, bf16[192,896]{1,0:T(8,128)(2,1)S(1)}, u32[]{:S(2)}) copy-start(bf16[192,896]{1,0:T(8,128)(2,1)S(1)} %get-tuple-element.4) | copy-start | bytes 1032196
where the time goes:
time: 99.7 us; the launch traced here: 98.5 us
  waiting for transfers between devices  50 us (50%)
  starting transfers between devices  34.3 us (34%)
  local copies, waits for them, and re-layouts  8.96 us (9%)
  matrix products  2.53 us (3%)
  other arithmetic  2.06 us (2%)
    all_to_all x1, waiting for transfers between devices, per_device(): lax.all_to_all(outgoing, 'vocab', split_axis=0, concat_axis=0, tiled=True)  21.2 us
    all_to_all x1, waiting for transfers between devices, per_device(): lax.all_to_all(grad_out, 'width', split_axis=1, concat_axis=0, tiled=True)  20.4 us
    all_to_all x1, starting transfers between devices, per_device(): lax.all_to_all(slot_list, 'vocab', split_axis=0, concat_axis=0, tiled=True)  13.8 us
    all_to_all x1, starting transfers between devices, per_device(): lax.all_to_all(grad_out, 'width', split_axis=1, concat_axis=0, tiled=True)  13.1 us
    all_to_all x1, waiting for transfers between devices, per_device(): lax.all_to_all(slot_list, 'vocab', split_axis=0, concat_axis=0, tiled=True)  8.37 us
    all_to_all x1, starting transfers between devices, per_device(): lax.all_to_all(outgoing, 'vocab', split_axis=0, concat_axis=0, tiled=True)  7.36 us
    unnamed x16, local copies, waits for them, and re-layouts  4.43 us
    all_to_all x1, local copies, waits for them, and re-layouts, per_device(): lax.all_to_all(grad_out, 'width', split_axis=1, concat_axis=0, tiled=True)  2.65 us
  transfers between devices with their start and end apart: 3, of which 3 were waited for; matrix products, arithmetic and copies ran while one was open for 6% of the time, Pallas kernels for 0%

commit v1 on v0

v1 whole, which is shorter than its diff:
```python
import functools

import jax
import jax.numpy as jnp
from jax import lax
from jax.experimental import pallas as pl
from jax.experimental.pallas import tpu as pltpu
from jax.sharding import Mesh, PartitionSpec as P

BETA_ONE = 0.9
BETA_TWO = 0.95
LEARN_RATE = 0.01
WEIGHT_DECAY = 0.1
EPSILON = 1e-08
CORRECT_ONE = 1.0 - 0.9**10
CORRECT_TWO = 1.0 - 0.95**10
CAP = 2
LANES = 128


def adamw_rows(param, moment1, moment2, table_grad):
    first_full = BETA_ONE * moment1.astype(jnp.float32) + (1.0 - BETA_ONE) * table_grad
    second_full = (
        BETA_TWO * moment2.astype(jnp.float32) + (1.0 - BETA_TWO) * table_grad * table_grad
    )
    new_moment1 = lax.optimization_barrier(first_full.astype(jnp.bfloat16))
    new_moment2 = lax.optimization_barrier(second_full.astype(jnp.bfloat16))
    first_round = new_moment1.astype(jnp.float32)
    second_round = new_moment2.astype(jnp.float32)
    update = first_round / CORRECT_ONE / (jnp.sqrt(second_round / CORRECT_TWO) + EPSILON)
    new_param = param - LEARN_RATE * (update + WEIGHT_DECAY * param)
    return (new_param, new_moment1, new_moment2)


def chip_sums_kernel(block_rows, tokens_ref, slots_ref, own_ref, other_ref, out_ref, rows_ref, held, sems):
    x, c = lax.axis_index("x"), lax.axis_index("c")
    parts, groups, pair = out_ref.shape
    cols = pair // CAP
    half = own_ref.shape[0]
    copies = []
    for p in range(parts):
        start = pl.multiple_of((2 * p + c) * cols, LANES)
        for h, ref in enumerate((own_ref, other_ref)):
            copy = pltpu.make_async_copy(
                ref.at[:, pl.ds(start, cols)], held.at[p, pl.ds(h * half, half), :], sems.at[p, h]
            )
            copy.start()
            copies.append(copy)
    slots = slots_ref[...]
    wide = jnp.broadcast_to(slots, (groups, slots.shape[1]))
    row = lax.broadcasted_iota(jnp.int32, wide.shape, 0)
    lane = lax.broadcasted_iota(jnp.int32, wide.shape, 1)
    columns = [
        jnp.sum(jnp.where(lane == CAP * row + k, wide, 0), axis=1, keepdims=True) for k in range(CAP)
    ]
    first = 2 * x * half
    own_ids = tokens_ref[:, pl.ds(pl.multiple_of(first + c * half, LANES), half)]
    other_ids = tokens_ref[:, pl.ds(pl.multiple_of(first + (1 - c) * half, LANES), half)]
    ids = jnp.concatenate([own_ids, other_ids], axis=1)
    hots = [(col == ids).astype(jnp.float32).astype(jnp.bfloat16) for col in columns]
    base = lax.broadcasted_iota(jnp.int32, (groups, LANES), 0) * block_rows
    which = lax.broadcasted_iota(jnp.int32, (groups, LANES), 1)
    local = jnp.where(which == 0, columns[0], columns[1])
    local = jnp.where(local < 0, -1, local - base)
    rows_ref[...] = local.astype(jnp.float32).astype(jnp.bfloat16)
    for p in range(parts):
        copies[2 * p].wait()
        copies[2 * p + 1].wait()
        for k in range(CAP):
            out_ref[p, :, k * cols : (k + 1) * cols] = jnp.dot(
                hots[k], held[p], preferred_element_type=jnp.float32
            ).astype(jnp.bfloat16)


def chip_sums(token_ids, slot_ids, own, other, parts, block_rows):
    half, width = own.shape
    cols = width // (2 * parts)
    slots = slot_ids.shape[1]
    groups = slots // CAP
    vmem = pl.BlockSpec(memory_space=pltpu.VMEM)
    hbm = pl.BlockSpec(memory_space=pl.ANY)
    return pl.pallas_call(
        functools.partial(chip_sums_kernel, block_rows),
        out_shape=(
            jax.ShapeDtypeStruct((parts, groups, CAP * cols), jnp.bfloat16),
            jax.ShapeDtypeStruct((groups, LANES), jnp.bfloat16),
        ),
        in_specs=[vmem, vmem, hbm, hbm],
        out_specs=(vmem, vmem),
        scratch_shapes=[
            pltpu.VMEM((parts, 2 * half, cols), jnp.bfloat16),
            pltpu.SemaphoreType.DMA((parts, 2)),
        ],
        compiler_params=pltpu.CompilerParams(vmem_limit_bytes=24 * 1024 * 1024),
    )(token_ids.reshape(1, -1), slot_ids, own, other)


def per_device(grad_out, token_ids, slot_ids, param, moment1, moment2):
    block_rows, cols = param.shape
    parts = grad_out.shape[1] // (2 * cols)
    groups = slot_ids.shape[1] // CAP
    other = lax.ppermute(grad_out, "c", [(0, 1), (1, 0)])
    sums, rows = chip_sums(token_ids, slot_ids, grad_out, other, parts, block_rows)
    arrived = lax.all_to_all(sums, "x", split_axis=0, concat_axis=0, tiled=True)
    total = jnp.sum(arrived.astype(jnp.float32), axis=0).astype(jnp.bfloat16)
    outgoing = jnp.concatenate([total, rows], axis=1)[:, None, :]
    slot_sums = lax.all_to_all(outgoing, "vocab", split_axis=0, concat_axis=0, tiled=True)
    slot_sums = slot_sums.reshape(groups, -1)
    table_grad = jnp.zeros((block_rows, cols), jnp.float32)
    for k in range(CAP):
        named = slot_sums[:, CAP * cols + k].astype(jnp.int32)
        selector = (named[:, None] == lax.iota(jnp.int32, block_rows)[None, :]).astype(jnp.bfloat16)
        table_grad += lax.dot_general(
            selector,
            slot_sums[:, k * cols : (k + 1) * cols],
            (((0,), (0,)), ((), ())),
            preferred_element_type=jnp.float32,
        )
    return adamw_rows(param, moment1, moment2, table_grad)


def solution(mesh):
    vocab, width = mesh.devices.shape
    split = Mesh(mesh.devices.reshape(vocab, width // 2, 2), ("vocab", "x", "c"))
    slab = P("vocab", ("x", "c"))
    return jax.shard_map(
        per_device,
        mesh=split,
        in_specs=(P(("vocab", "x", "c"), None), P("vocab"), P("vocab", None), slab, slab, slab),
        out_specs=(slab, slab, slab),
        check_vma=False,
    )
```

time: 99.7 us -> 83.5 us (0.84)
  blocking collectives: 0 us -> 66.4 us
  waiting for transfers between devices: 50 us -> 3.96 us
  starting transfers between devices: 34.3 us -> 1.92 us
  local copies, waits for them, and re-layouts: 8.96 us -> 4.36 us
  matrix products: 2.53 us -> 0.85 us
  Pallas kernels: 0 us -> 1.67 us
    all_to_all x0 -> x2, blocking collectives: none -> 66.4 us  [the longest x1 37.4 us: per_device(): lax.all_to_all(outgoing, 'vocab', split_axis=0, concat_axis=0, tiled=True)]
    all_to_all x3 -> x0, waiting for transfers between devices: 50 us -> none  [the longest x1 21.2 us: per_device(): lax.all_to_all(outgoing, 'vocab', split_axis=0, concat_axis=0, tiled=True)]
    all_to_all x3 -> x0, starting transfers between devices: 34.3 us -> none  [the longest x1 13.8 us: per_device(): lax.all_to_all(slot_list, 'vocab', split_axis=0, concat_axis=0, tiled=True)]
    all_to_all x4 -> x0, local copies, waits for them, and re-layouts: 4.4 us -> none  [the longest x1 2.65 us: per_device(): lax.all_to_all(grad_out, 'width', split_axis=1, concat_axis=0, tiled=True)]
    ppermute x0 -> x1, waiting for transfers between devices: none -> 3.96 us  [per_device(): other = lax.ppermute(grad_out, 'c', [(0, 1), (1, 0)])]
    ppermute x0 -> x1, starting transfers between devices: none -> 1.92 us  [per_device(): other = lax.ppermute(grad_out, 'c', [(0, 1), (1, 0)])]
    dot_general x2, matrix products: 2.53 us -> 0.85 us  [per_device(): lax.dot_general(selector, slot_sums[:, k * cols:(k + 1) * cols], (((0,),...]
    pallas_call x0 -> x1, Pallas kernels: none -> 1.67 us  [chip_sums(): pl.pallas_call(functools.partial(chip_sums_kernel, block_rows), out_shape...]
  transfers between devices with their start and end apart: 3 -> 1, of which waited for: 3 -> 1; matrix products, arithmetic and copies ran while one was open for 6% -> 0% of each run, Pallas kernels for 0% -> 0%
where the time goes in v1:
time: 83.5 us; the launch traced here: 82.5 us
  blocking collectives  66.4 us (80%)
  local copies, waits for them, and re-layouts  4.36 us (5%)
  waiting for transfers between devices  3.96 us (5%)
  other arithmetic  2.53 us (3%)
  starting transfers between devices  1.92 us (2%)
  Pallas kernels  1.67 us (2%)
  matrix products  0.85 us (1%)
    all_to_all x1, blocking collectives, per_device(): lax.all_to_all(outgoing, 'vocab', split_axis=0, concat_axis=0, tiled=True)  37.4 us
    all_to_all x1, blocking collectives, per_device(): arrived = lax.all_to_all(sums, 'x', split_axis=0, concat_axis=0, tiled=True)  29 us
    ppermute x1, waiting for transfers between devices, per_device(): other = lax.ppermute(grad_out, 'c', [(0, 1), (1, 0)])  3.96 us
    unnamed x19, local copies, waits for them, and re-layouts  3.85 us
    ppermute x1, starting transfers between devices, per_device(): other = lax.ppermute(grad_out, 'c', [(0, 1), (1, 0)])  1.92 us
    pallas_call x1, Pallas kernels, chip_sums(): pl.pallas_call(functools.partial(chip_sums_kernel, block_rows), out_shape...  1.67 us
  transfers between devices with their start and end apart: 1, of which 1 were waited for; matrix products, arithmetic and copies ran while one was open for 0% of the time, Pallas kernels for 0%

profile of v1, /device:TPU:6, one launch (start us, length us, event | category | flops | bytes accessed | tf_op | source)
XLA Modules:
  0.0 82.5 jit_solution(9586256685579000968)
XLA Ops:
  0.6 1.9 %collective-permute-start = (bf16[128,7168]{1,0:T(8,128)(2,1)}, bf16[128,7168]{1,0:T(8,128)(2,1)S(1)}, u32[]{:S(2)}, u32[]{:S(2)}) collective-permute-start(bf16[128,7168]{1,0:T(8,128)(2,1)} %own_ref.1), channel_id=1, source_target_pairs={{0,1},{1,0},{2,3},{3,2},{4,5},{5,4},{6,7},{7,6},{8,9},{9,8},{10,11... | collective-permute-start | bytes 5505032 | tf_op jit(solution)/shard_map/ppermute | solution.py:102
  2.6 4.0 %collective-permute-done.other_ref = bf16[128,7168]{1,0:T(8,128)(2,1)S(1)} collective-permute-done((bf16[128,7168]{1,0:T(8,128)(2,1)}, bf16[128,7168]{1,0:T(8,128)(2,1)S(1)}, u32[]{:S(2)}, u32[]{:S(2)}) %collective-permute-start) | collective-permute-done | bytes 1835040 | tf_op jit(solution)/shard_map/ppermute | solution.py:102
  6.5 0.0 copy-start
  6.5 1.5 %copy-done = bf16[128,7168]{1,0:T(8,128)(2,1)S(1)} copy-done((bf16[128,7168]{1,0:T(8,128)(2,1)S(1)}, bf16[128,7168]{1,0:T(8,128)(2,1)}, u32[]{:S(2)}) %copy-start) | copy-done | bytes 1835032
  8.0 0.0 copy-start.1
  8.0 0.7 copy-done.1
  8.7 0.0 copy-start.2
  8.7 0.7 copy-done.2
  9.4 1.7 %shard_map.85 = (bf16[4,96,1792]{2,1,0:T(8,128)(2,1)S(1)}, bf16[96,128]{1,0:T(8,128)(2,1)S(1)}) custom-call(s32[1,1024]{1,0:T(1,128)S(1)} %bitcast.6, s32[1,192]{1,0:T(1,128)S(1)} %copy-done.2, bf16[128,7168]{1,0:T(8,128)(2,1)S(1)} %copy-done, bf16[128,7168]{1,0:T(8,128)(2,1)S(1)} %collective-permute-done.other_ref), custom_call_target="tpu_custom_call" | custom-call | tf_op jit(solution)/shard_map/pallas_call | solution.py:82
  11.1 29.0 %all_to_all.10 = bf16[4,96,1792]{2,1,0:T(8,128)(2,1)S(1)} all-to-all(bf16[4,96,1792]{2,1,0:T(8,128)(2,1)S(1)} %get-tuple-element.5), channel_id=1, replica_groups=mesh['vocab'=96,'x'=4,'c'=2] {'x'}, dimensions={0} | all-to-all | bytes 2752512 | tf_op jit(solution)/shard_map/all_to_all | solution.py:104
  40.1 0.2 reduce_sum.12
  40.4 0.5 broadcast.10
  40.9 0.8 %reduce.5 = bf16[96,1920]{1,0:T(8,128)(2,1)S(1)} reduce(bf16[96,1,1920]{2,0,1:T(8,128)(2,1)S(1)} %maximum_bitcast_fusion, bf16[]{:T(256)} %broadcast.10), dimensions={1}, to_apply=%copy.11.reduce_sub_computation | reduce | bytes 737282 | tf_op jit(solution)/shard_map/broadcast_in_dim | solution.py:106
  41.7 0.4 reshape.18
  42.1 0.0 copy-start.6
  42.1 0.0 copy-start.7
  42.1 37.4 %all_to_all.11 = bf16[96,2,960]{2,1,0:T(2,128)(2,1)S(1)} all-to-all(bf16[96,2,960]{2,1,0:T(2,128)(2,1)S(1)} %reshape.18), channel_id=1, replica_groups=mesh['vocab'=96,'x'=4,'c'=2] {'vocab'}, dimensions={0} | all-to-all | bytes 737280 | tf_op jit(solution)/shard_map/all_to_all | solution.py:107
  79.5 0.5 reshape.19
  80.1 0.0 copy-start.5
  80.1 0.2 convert_reduce_fusion
  80.3 0.4 fusion.3
  80.6 0.0 copy-done.6
  80.6 0.0 copy-done.7
  80.7 0.5 add_convert_fusion
  81.2 0.0 copy-start.3
  81.2 0.0 copy-start.4
  81.2 0.0 copy-done.5
  81.2 1.3 %multiply_subtract_fusion = f32[192,896]{1,0:T(8,128)} fusion(f32[192,896]{1,0:T(8,128)S(1)} %copy-done.5, bf16[192,896]{1,0:T(8,128)(2,1)S(1)} %get-tuple-element.10, bf16[192,896]{1,0:T(8,128)(2,1)S(1)} %get-tuple-element.9), kind=kLoop, calls=%fused_computation.4 | loop fusion | flops 1720320 | bytes 2064384 | tf_op jit(solution)/shard_map/sub | solution.py:31
  82.4 0.0 copy-done.3
  82.4 0.0 copy-done.4
  (2 shorter events, 0.1 us)
Async XLA Ops:
  0.6 5.9 %collective-permute-start = (bf16[128,7168]{1,0:T(8,128)(2,1)}, bf16[128,7168]{1,0:T(8,128)(2,1)S(1)}, u32[]{:S(2)}, u32[]{:S(2)}) collective-permute-start(bf16[128,7168]{1,0:T(8,128)(2,1)} %own_ref.1), channel_id=1, source_target_pairs={{0,1},{1,0},{2,3},{3,2},{4,5},{5,4},{6,7},{7,6},{8,9},{9,8},{10,11... | collective-permute-start | bytes 5505032 | tf_op jit(solution)/shard_map/ppermute | solution.py:102
  6.5 1.5 %copy-start = (bf16[128,7168]{1,0:T(8,128)(2,1)S(1)}, bf16[128,7168]{1,0:T(8,128)(2,1)}, u32[]{:S(2)}) copy-start(bf16[128,7168]{1,0:T(8,128)(2,1)} %own_ref.1) | copy-start | bytes 5505028
  8.0 0.7 copy-start.1
  8.7 0.7 copy-start.2
  42.1 38.5 %copy-start.6 = (bf16[192,896]{1,0:T(8,128)(2,1)S(1)}, bf16[192,896]{1,0:T(8,128)(2,1)}, u32[]{:S(2)}) copy-start(bf16[192,896]{1,0:T(8,128)(2,1)} %param.10) | copy-start | bytes 1032196
  42.1 38.5 %copy-start.7 = (bf16[192,896]{1,0:T(8,128)(2,1)S(1)}, bf16[192,896]{1,0:T(8,128)(2,1)}, u32[]{:S(2)}) copy-start(bf16[192,896]{1,0:T(8,128)(2,1)} %param.11) | copy-start | bytes 1032196
  80.1 1.1 %copy-start.5 = (f32[192,896]{1,0:T(8,128)S(1)}, f32[192,896]{1,0:T(8,128)}, u32[]{:S(2)}) copy-start(f32[192,896]{1,0:T(8,128)} %param.9) | copy-start | bytes 2064388
  81.2 1.3 %copy-start.3 = (bf16[192,896]{1,0:T(8,128)(2,1)}, bf16[192,896]{1,0:T(8,128)(2,1)S(1)}, u32[]{:S(2)}) copy-start(bf16[192,896]{1,0:T(8,128)(2,1)S(1)} %get-tuple-element.9) | copy-start | bytes 1032196
  81.2 1.3 %copy-start.4 = (bf16[192,896]{1,0:T(8,128)(2,1)}, bf16[192,896]{1,0:T(8,128)(2,1)S(1)}, u32[]{:S(2)}) copy-start(bf16[192,896]{1,0:T(8,128)(2,1)S(1)} %get-tuple-element.10) | copy-start | bytes 1032196

commit v2 on v0

v2 whole, which is shorter than its diff:
```python
import jax
import jax.numpy as jnp
from jax import lax
from jax.experimental import pallas as pl
from jax.experimental.pallas import tpu as pltpu
from jax.sharding import Mesh, PartitionSpec as P

BETA_ONE = 0.9
BETA_TWO = 0.95
LEARN_RATE = 0.01
WEIGHT_DECAY = 0.1
EPSILON = 1e-08
CORRECT_ONE = 1.0 - 0.9**10
CORRECT_TWO = 1.0 - 0.95**10
CAP = 2
LANES = 128
VMEM = pl.BlockSpec(memory_space=pltpu.VMEM)
HBM = pl.BlockSpec(memory_space=pltpu.HBM)


def one_hot(mask):
    return mask.astype(jnp.float32).astype(jnp.bfloat16)


def setup_kernel(block_rows, tokens_ref, slots_ref, grad_ref, hot_ref, rows_ref, own_ref, tokens, slot_row, sems):
    x, c = lax.axis_index("x"), lax.axis_index("c")
    parts, half, cols = own_ref.shape
    slots = slot_row.shape[1]
    first = pl.multiple_of(2 * x * half, LANES)
    small = [
        pltpu.make_async_copy(tokens_ref.at[:, pl.ds(first, 2 * half)], tokens, sems.at[parts]),
        pltpu.make_async_copy(slots_ref, slot_row, sems.at[parts + 1]),
    ]
    large = []
    for k in range(parts):
        start = pl.multiple_of((2 * lax.rem(x + k, parts) + c) * cols, LANES)
        large.append(pltpu.make_async_copy(grad_ref.at[:, pl.ds(start, cols)], own_ref.at[k], sems.at[k]))
    for copy in small + large:
        copy.start()
    for copy in small:
        copy.wait()
    row = lax.broadcasted_iota(jnp.int32, (slots, slots), 0)
    lane = lax.broadcasted_iota(jnp.int32, (slots, slots), 1)
    wide = jnp.broadcast_to(slot_row[...], (slots, slots))
    column = jnp.sum(jnp.where(lane == row, wide, 0), axis=1, keepdims=True)
    low, high = tokens[:, :half], tokens[:, half:]
    hot_ref[:, :half] = one_hot(column == jnp.where(c == 0, low, high))
    hot_ref[:, half:] = one_hot(column == jnp.where(c == 0, high, low))
    block = lax.broadcasted_iota(jnp.int32, (slots, LANES), 0) // CAP
    local = jnp.where(column < 0, -1, column - block * block_rows)
    rows_ref[...] = local.astype(jnp.float32).astype(jnp.bfloat16)
    for copy in large:
        copy.wait()


def chip_sums_kernel(hot_ref, own_ref, other_ref, *out_refs):
    x, c = lax.axis_index("x"), lax.axis_index("c")
    parts, half, cols = own_ref.shape
    for k in (2, 1, 3, 0) if parts == 4 else range(parts):
        start = pl.multiple_of((2 * lax.rem(x + k, parts) + c) * cols, LANES)
        tokens = jnp.concatenate([own_ref[k], other_ref[:, pl.ds(start, cols)]], axis=0)
        out_refs[k][...] = jnp.dot(hot_ref[...], tokens, preferred_element_type=jnp.float32).astype(jnp.bfloat16)


def group_sums_kernel(rows_ref, *refs):
    parts, out_ref = refs[:-1], refs[-1]
    cols = parts[0].shape[1]
    total = parts[0][...].astype(jnp.float32)
    for ref in parts[1:]:
        total += ref[...].astype(jnp.float32)
    out_ref[:, :cols] = total.astype(jnp.bfloat16)
    out_ref[:, cols:] = rows_ref[...]


def update_kernel(sums_ref, param_ref, first_ref, second_ref, *refs):
    outs, (param_buf, first_buf, second_buf, sems) = refs[:3], refs[3:]
    block_rows, cols = param_ref.shape
    names = sums_ref[:, cols:].astype(jnp.int32)
    row = lax.broadcasted_iota(jnp.int32, names.shape, 1)
    pieces = [one_hot(names == row + start) for start in range(0, block_rows, LANES)]
    selector = jnp.concatenate(pieces, axis=1)
    copies = []
    step = 2 * LANES if cols % (2 * LANES) == 0 else LANES
    step = cols // 7 * 2 if cols % (7 * LANES) == 0 else step
    edges = list(range(0, cols, step)) + [cols]
    for i, (lo, hi) in enumerate(zip(edges[:-1], edges[1:])):
        table_grad = lax.dot_general(
            selector, sums_ref[:, lo:hi], (((0,), (0,)), ((), ())), preferred_element_type=jnp.float32
        )[:block_rows]
        first = BETA_ONE * first_ref[:, lo:hi].astype(jnp.float32) + (1.0 - BETA_ONE) * table_grad
        second = BETA_TWO * second_ref[:, lo:hi].astype(jnp.float32) + (1.0 - BETA_TWO) * table_grad * table_grad
        first, second = first.astype(jnp.bfloat16), second.astype(jnp.bfloat16)
        first_buf[:, lo:hi] = first
        second_buf[:, lo:hi] = second
        scale = jnp.sqrt(second.astype(jnp.float32) * (1.0 / CORRECT_TWO)) + EPSILON
        change = first.astype(jnp.float32) * (1.0 / CORRECT_ONE) / scale
        old = param_ref[:, lo:hi]
        param_buf[:, lo:hi] = old - LEARN_RATE * (change + WEIGHT_DECAY * old)
        for j, (buf, out) in enumerate(zip((param_buf, first_buf, second_buf), outs)):
            copy = pltpu.make_async_copy(buf.at[:, pl.ds(lo, hi - lo)], out.at[:, pl.ds(lo, hi - lo)], sems.at[i, j])
            copy.start()
            copies.append(copy)
    for copy in copies:
        copy.wait()


def per_device(grad_out, token_ids, slot_ids, param, moment1, moment2):
    half = grad_out.shape[0]
    block_rows, cols = param.shape
    parts = grad_out.shape[1] // (2 * cols)
    slots = slot_ids.shape[1]
    bf16, f32 = jnp.bfloat16, jnp.float32
    limit = pltpu.CompilerParams(vmem_limit_bytes=24 * 1024 * 1024)

    other = lax.ppermute(grad_out, "c", [(0, 1), (1, 0)])
    hot, rows, own = pl.pallas_call(
        lambda *refs: setup_kernel(block_rows, *refs),
        out_shape=(
            jax.ShapeDtypeStruct((slots, 2 * half), bf16),
            jax.ShapeDtypeStruct((slots, LANES), bf16),
            jax.ShapeDtypeStruct((parts, half, cols), bf16),
        ),
        in_specs=[HBM] * 3,
        out_specs=(VMEM,) * 3,
        scratch_shapes=[
            pltpu.VMEM((1, 2 * half), jnp.int32),
            pltpu.VMEM((1, slots), jnp.int32),
            pltpu.SemaphoreType.DMA((parts + 2,)),
        ],
        compiler_params=limit,
        cost_estimate=pl.CostEstimate(flops=10**6, bytes_accessed=4 * 10**6, transcendentals=0),
        name="setup",
    )(token_ids.reshape(1, -1), slot_ids, grad_out)
    sums = pl.pallas_call(
        chip_sums_kernel,
        out_shape=(jax.ShapeDtypeStruct((slots, cols), bf16),) * parts,
        in_specs=[VMEM] * 3,
        out_specs=(VMEM,) * parts,
        compiler_params=limit,
        name="chip_sums",
    )(hot, own, other)
    arrived = [sums[0]]
    for k in range(1, parts):
        arrived.append(lax.ppermute(sums[k], "x", [(i, (i + k) % parts) for i in range(parts)]))
    outgoing = pl.pallas_call(
        group_sums_kernel,
        out_shape=jax.ShapeDtypeStruct((slots, cols + LANES), bf16),
        in_specs=[VMEM] * (parts + 1),
        out_specs=VMEM,
        compiler_params=limit,
        name="group_sums",
    )(rows, *arrived)
    outgoing = outgoing.reshape(slots // CAP, CAP, cols + LANES)
    slot_sums = lax.all_to_all(outgoing, "vocab", split_axis=0, concat_axis=0, tiled=True)
    slot_sums = slot_sums.reshape(slots, cols + LANES)
    chunks = 8
    return tuple(
        pl.pallas_call(
            update_kernel,
            out_shape=(
                jax.ShapeDtypeStruct(param.shape, f32),
                jax.ShapeDtypeStruct(param.shape, bf16),
                jax.ShapeDtypeStruct(param.shape, bf16),
            ),
            in_specs=[VMEM] * 4,
            out_specs=(HBM,) * 3,
            scratch_shapes=[
                pltpu.VMEM(param.shape, f32),
                pltpu.VMEM(param.shape, bf16),
                pltpu.VMEM(param.shape, bf16),
                pltpu.SemaphoreType.DMA((chunks, 3)),
            ],
            compiler_params=limit,
            name="update",
        )(slot_sums, param, moment1, moment2)
    )


def solution(mesh):
    vocab, width = mesh.devices.shape
    split = Mesh(mesh.devices.reshape(vocab, width // 2, 2), ("vocab", "x", "c"))
    slab = P("vocab", ("x", "c"))
    return jax.shard_map(
        per_device,
        mesh=split,
        in_specs=(P(("vocab", "x", "c"), None), P("vocab"), P("vocab", None), slab, slab, slab),
        out_specs=(slab, slab, slab),
        check_vma=False,
    )
```

time: 99.7 us -> 79.8 us (0.80)
  blocking collectives: 0 us -> 36.9 us
  waiting for transfers between devices: 50 us -> 16.6 us
  starting transfers between devices: 34.3 us -> 18 us
  local copies, waits for them, and re-layouts: 8.96 us -> 3.17 us
  Pallas kernels: 0 us -> 3 us
  matrix products: 2.53 us -> 0 us
  other arithmetic: 2.06 us -> 0 us
    all_to_all x3 -> x0, waiting for transfers between devices: 50 us -> none  [the longest x1 21.2 us: per_device(): lax.all_to_all(outgoing, 'vocab', split_axis=0, concat_axis=0, tiled=True)]
    all_to_all x0 -> x1, blocking collectives: none -> 36.9 us  [per_device(): lax.all_to_all(outgoing, 'vocab', split_axis=0, concat_axis=0, tiled=True)]
    all_to_all x3 -> x0, starting transfers between devices: 34.3 us -> none  [the longest x1 13.8 us: per_device(): lax.all_to_all(slot_list, 'vocab', split_axis=0, concat_axis=0, tiled=True)]
    ppermute x0 -> x4, starting transfers between devices: none -> 18 us  [the longest x3 16.1 us: per_device(): lax.ppermute(sums[k], 'x', [(i, (i + k) % parts) for i in range(parts)])]
    ppermute x0 -> x4, waiting for transfers between devices: none -> 16.6 us  [the longest x3 15.9 us: per_device(): lax.ppermute(sums[k], 'x', [(i, (i + k) % parts) for i in range(parts)])]
    all_to_all x4 -> x0, local copies, waits for them, and re-layouts: 4.4 us -> none  [the longest x1 2.65 us: per_device(): lax.all_to_all(grad_out, 'width', split_axis=1, concat_axis=0, tiled=True)]
    pallas_call x0 -> x4, Pallas kernels: none -> 3 us  [the longest x1 1.88 us: per_device(): pl.pallas_call(update_kernel, out_shape=(jax.ShapeDtypeStruct(param.shape...]
    dot_general x2 -> x0, matrix products: 2.53 us -> none  [the longest x1 2.18 us: per_device(): summed = jnp.dot(onehot, regrouped, preferred_element_type=jnp.float32)]
  transfers between devices with their start and end apart: 3 -> 4, of which waited for: 3 -> 3; matrix products, arithmetic and copies ran while one was open for 6% -> 0% of each run, Pallas kernels for 0% -> 0%
where the time goes in v2:
time: 79.8 us; the launch traced here: 78.4 us
  blocking collectives  36.9 us (46%)
  starting transfers between devices  18 us (23%)
  waiting for transfers between devices  16.6 us (21%)
  local copies, waits for them, and re-layouts  3.17 us (4%)
  Pallas kernels  3 us (4%)
    all_to_all x1, blocking collectives, per_device(): lax.all_to_all(outgoing, 'vocab', split_axis=0, concat_axis=0, tiled=True)  36.9 us
    ppermute x3, starting transfers between devices, per_device(): lax.ppermute(sums[k], 'x', [(i, (i + k) % parts) for i in range(parts)])  16.1 us
    ppermute x3, waiting for transfers between devices, per_device(): lax.ppermute(sums[k], 'x', [(i, (i + k) % parts) for i in range(parts)])  15.9 us
    unnamed x12, local copies, waits for them, and re-layouts  2.87 us
    ppermute x1, starting transfers between devices, per_device(): other = lax.ppermute(grad_out, 'c', [(0, 1), (1, 0)])  1.92 us
    pallas_call x1, Pallas kernels, per_device(): pl.pallas_call(update_kernel, out_shape=(jax.ShapeDtypeStruct(param.shape...  1.88 us
  transfers between devices with their start and end apart: 4, of which 3 were waited for; matrix products, arithmetic and copies ran while one was open for 0% of the time, Pallas kernels for 0%

profile of v2, /device:TPU:6, one launch (start us, length us, event | category | flops | bytes accessed | tf_op | source)
XLA Modules:
  0.0 78.4 jit_solution(6023336913815653492)
XLA Ops:
  0.6 1.9 %collective-permute-start = (bf16[128,7168]{1,0:T(8,128)(2,1)}, bf16[128,7168]{1,0:T(8,128)(2,1)S(1)}, u32[]{:S(2)}, u32[]{:S(2)}) collective-permute-start(bf16[128,7168]{1,0:T(8,128)(2,1)} %refs_2_.1), channel_id=1, source_target_pairs={{0,1},{1,0},{2,3},{3,2},{4,5},{5,4},{6,7},{7,6},{8,9},{9,8},{10,11... | collective-permute-start | bytes 5505032 | tf_op jit(solution)/shard_map/ppermute | solution.py:115
  2.6 0.0 copy-start
  2.6 1.5 %copy-done = bf16[128,7168]{1,0:T(8,128)(2,1)S(1)} copy-done((bf16[128,7168]{1,0:T(8,128)(2,1)S(1)}, bf16[128,7168]{1,0:T(8,128)(2,1)}, u32[]{:S(2)}) %copy-start) | copy-done | bytes 1835032
  4.1 0.0 copy-start.4
  4.1 0.7 copy-done.4
  4.7 0.0 copy-start.5
  4.7 0.7 copy-done.5
  5.4 0.3 setup.1
  5.8 0.7 collective-permute-done.other_ref
  6.5 0.6 chip_sums.1
  7.1 11.4 %collective-permute-start.1 = (bf16[192,896]{1,0:T(8,128)(2,1)S(1)}, bf16[192,896]{1,0:T(8,128)(2,1)S(1)}, u32[]{:S(2)}, u32[]{:S(2)}) collective-permute-start(bf16[192,896]{1,0:T(8,128)(2,1)S(1)} %get-tuple-element.14), channel_id=1, source_target_pairs={{0,2},{2,4},{4,6},{6,0},{1,3},{3,5},{5,7},{7,1},{8,10},{10,12},{12... | collective-permute-start | bytes 1032200 | tf_op jit(solution)/shard_map/ppermute | solution.py:144
  18.5 1.9 %collective-permute-start.2 = (bf16[192,896]{1,0:T(8,128)(2,1)S(1)}, bf16[192,896]{1,0:T(8,128)(2,1)S(1)}, u32[]{:S(2)}, u32[]{:S(2)}) collective-permute-start(bf16[192,896]{1,0:T(8,128)(2,1)S(1)} %get-tuple-element.15), channel_id=1, source_target_pairs={{0,4},{2,6},{4,0},{6,2},{1,5},{3,7},{5,1},{7,3},{8,12},{10,14},{12... | collective-permute-start | bytes 1032200 | tf_op jit(solution)/shard_map/ppermute | solution.py:144
  20.5 2.8 %collective-permute-start.3 = (bf16[192,896]{1,0:T(8,128)(2,1)S(1)}, bf16[192,896]{1,0:T(8,128)(2,1)S(1)}, u32[]{:S(2)}, u32[]{:S(2)}) collective-permute-start(bf16[192,896]{1,0:T(8,128)(2,1)S(1)} %get-tuple-element.16), channel_id=1, source_target_pairs={{0,6},{2,0},{4,2},{6,4},{1,7},{3,1},{5,3},{7,5},{8,14},{10,8},{12,... | collective-permute-start | bytes 1032200 | tf_op jit(solution)/shard_map/ppermute | solution.py:144
  23.2 10.3 %collective-permute-done.1.refs_1_ = bf16[192,896]{1,0:T(8,128)(2,1)S(1)} collective-permute-done((bf16[192,896]{1,0:T(8,128)(2,1)S(1)}, bf16[192,896]{1,0:T(8,128)(2,1)S(1)}, u32[]{:S(2)}, u32[]{:S(2)}) %collective-permute-start.1) | collective-permute-done | bytes 344096 | tf_op jit(solution)/shard_map/ppermute | solution.py:144
  33.5 0.0 collective-permute-done.2.refs_2_
  33.5 5.6 %collective-permute-done.3.refs_3_ = bf16[192,896]{1,0:T(8,128)(2,1)S(1)} collective-permute-done((bf16[192,896]{1,0:T(8,128)(2,1)S(1)}, bf16[192,896]{1,0:T(8,128)(2,1)S(1)}, u32[]{:S(2)}, u32[]{:S(2)}) %collective-permute-start.3) | collective-permute-done | bytes 344096 | tf_op jit(solution)/shard_map/ppermute | solution.py:144
  39.1 0.0 copy-start.1
  39.1 0.0 copy-start.2
  39.1 0.0 copy-start.3
  39.1 0.2 group_sums.1
  39.3 0.1 reshape.16
  39.5 36.9 %all_to_all.5 = bf16[96,2,1024]{2,1,0:T(2,128)(2,1)S(1)} all-to-all(bf16[96,2,1024]{2,1,0:T(2,128)(2,1)S(1)} %reshape.16), channel_id=1, replica_groups=mesh['vocab'=96,'x'=4,'c'=2] {'vocab'}, dimensions={0} | all-to-all | bytes 786432 | tf_op jit(solution)/shard_map/all_to_all | solution.py:154
  76.4 0.1 reshape.17.sums_ref
  76.5 0.0 copy-done.1
  76.5 0.0 copy-done.2
  76.6 0.0 copy-done.3
  76.6 1.9 %update.1 = (f32[192,896]{1,0:T(8,128)}, bf16[192,896]{1,0:T(8,128)(2,1)}, bf16[192,896]{1,0:T(8,128)(2,1)}) custom-call(bf16[192,1024]{1,0:T(8,128)(2,1)S(1)} %reshape.17.sums_ref, f32[192,896]{1,0:T(8,128)S(1)} %copy-done.1, bf16[192,896]{1,0:T(8,128)(2,1)S(1)} %copy-done.2, bf16[192,896]{1,0:T(8,128)(2,1)S(1)} %copy-done.3), custom_call_target="tpu_custom_call" | custom-call | tf_op jit(solution)/shard_map/update/pallas_call | solution.py:158
Async XLA Ops:
  0.6 5.9 %collective-permute-start = (bf16[128,7168]{1,0:T(8,128)(2,1)}, bf16[128,7168]{1,0:T(8,128)(2,1)S(1)}, u32[]{:S(2)}, u32[]{:S(2)}) collective-permute-start(bf16[128,7168]{1,0:T(8,128)(2,1)} %refs_2_.1), channel_id=1, source_target_pairs={{0,1},{1,0},{2,3},{3,2},{4,5},{5,4},{6,7},{7,6},{8,9},{9,8},{10,11... | collective-permute-start | bytes 5505032 | tf_op jit(solution)/shard_map/ppermute | solution.py:115
  2.6 1.5 %copy-start = (bf16[128,7168]{1,0:T(8,128)(2,1)S(1)}, bf16[128,7168]{1,0:T(8,128)(2,1)}, u32[]{:S(2)}) copy-start(bf16[128,7168]{1,0:T(8,128)(2,1)} %refs_2_.1) | copy-start | bytes 5505028
  4.1 0.7 copy-start.4
  4.7 0.7 copy-start.5
  7.1 26.4 %collective-permute-start.1 = (bf16[192,896]{1,0:T(8,128)(2,1)S(1)}, bf16[192,896]{1,0:T(8,128)(2,1)S(1)}, u32[]{:S(2)}, u32[]{:S(2)}) collective-permute-start(bf16[192,896]{1,0:T(8,128)(2,1)S(1)} %get-tuple-element.14), channel_id=1, source_target_pairs={{0,2},{2,4},{4,6},{6,0},{1,3},{3,5},{5,7},{7,1},{8,10},{10,12},{12... | collective-permute-start | bytes 1032200 | tf_op jit(solution)/shard_map/ppermute | solution.py:144
  18.5 15.0 %collective-permute-start.2 = (bf16[192,896]{1,0:T(8,128)(2,1)S(1)}, bf16[192,896]{1,0:T(8,128)(2,1)S(1)}, u32[]{:S(2)}, u32[]{:S(2)}) collective-permute-start(bf16[192,896]{1,0:T(8,128)(2,1)S(1)} %get-tuple-element.15), channel_id=1, source_target_pairs={{0,4},{2,6},{4,0},{6,2},{1,5},{3,7},{5,1},{7,3},{8,12},{10,14},{12... | collective-permute-start | bytes 1032200 | tf_op jit(solution)/shard_map/ppermute | solution.py:144
  20.5 18.7 %collective-permute-start.3 = (bf16[192,896]{1,0:T(8,128)(2,1)S(1)}, bf16[192,896]{1,0:T(8,128)(2,1)S(1)}, u32[]{:S(2)}, u32[]{:S(2)}) collective-permute-start(bf16[192,896]{1,0:T(8,128)(2,1)S(1)} %get-tuple-element.16), channel_id=1, source_target_pairs={{0,6},{2,0},{4,2},{6,4},{1,7},{3,1},{5,3},{7,5},{8,14},{10,8},{12,... | collective-permute-start | bytes 1032200 | tf_op jit(solution)/shard_map/ppermute | solution.py:144
  39.1 37.4 %copy-start.1 = (f32[192,896]{1,0:T(8,128)S(1)}, f32[192,896]{1,0:T(8,128)}, u32[]{:S(2)}) copy-start(f32[192,896]{1,0:T(8,128)} %param_ref.1) | copy-start | bytes 2064388
  39.1 37.4 %copy-start.2 = (bf16[192,896]{1,0:T(8,128)(2,1)S(1)}, bf16[192,896]{1,0:T(8,128)(2,1)}, u32[]{:S(2)}) copy-start(bf16[192,896]{1,0:T(8,128)(2,1)} %first_ref.1) | copy-start | bytes 1032196
  39.1 37.4 %copy-start.3 = (bf16[192,896]{1,0:T(8,128)(2,1)S(1)}, bf16[192,896]{1,0:T(8,128)(2,1)}, u32[]{:S(2)}) copy-start(bf16[192,896]{1,0:T(8,128)(2,1)} %second_ref.1) | copy-start | bytes 1032196

commit v3 on v2

--- a/solution.py
+++ b/solution.py
@@ -22,19 +22,29 @@
     return mask.astype(jnp.float32).astype(jnp.bfloat16)
 
 
+def chips(parts):
+    x, c = lax.axis_index("x"), lax.axis_index("c")
+    near, far = x ^ 1, x ^ (parts - 1)
+    return c, x, jnp.where(c == 0, near, far), jnp.where(c == 0, far, near), x ^ 2
+
+
+def block(chip, c, cols):
+    return pl.ds(pl.multiple_of((2 * chip + c) * cols, LANES), cols)
+
+
 def setup_kernel(block_rows, tokens_ref, slots_ref, grad_ref, hot_ref, rows_ref, own_ref, tokens, slot_row, sems):
-    x, c = lax.axis_index("x"), lax.axis_index("c")
     parts, half, cols = own_ref.shape
     slots = slot_row.shape[1]
+    c, x, partner, later, across = chips(parts)
     first = pl.multiple_of(2 * x * half, LANES)
     small = [
         pltpu.make_async_copy(tokens_ref.at[:, pl.ds(first, 2 * half)], tokens, sems.at[parts]),
         pltpu.make_async_copy(slots_ref, slot_row, sems.at[parts + 1]),
     ]
-    large = []
-    for k in range(parts):
-        start = pl.multiple_of((2 * lax.rem(x + k, parts) + c) * cols, LANES)
-        large.append(pltpu.make_async_copy(grad_ref.at[:, pl.ds(start, cols)], own_ref.at[k], sems.at[k]))
+    large = [
+        pltpu.make_async_copy(grad_ref.at[:, block(chip, c, cols)], own_ref.at[k], sems.at[k])
+        for k, chip in enumerate((partner, across, x, later))
+    ]
     for copy in small + large:
         copy.start()
     for copy in small:
@@ -46,28 +56,30 @@
     low, high = tokens[:, :half], tokens[:, half:]
     hot_ref[:, :half] = one_hot(column == jnp.where(c == 0, low, high))
     hot_ref[:, half:] = one_hot(column == jnp.where(c == 0, high, low))
-    block = lax.broadcasted_iota(jnp.int32, (slots, LANES), 0) // CAP
-    local = jnp.where(column < 0, -1, column - block * block_rows)
+    owner = lax.broadcasted_iota(jnp.int32, (slots, LANES), 0) // CAP
+    local = jnp.where(column < 0, -1, column - owner * block_rows)
     rows_ref[...] = local.astype(jnp.float32).astype(jnp.bfloat16)
     for copy in large:
         copy.wait()
 
 
-def chip_sums_kernel(hot_ref, own_ref, other_ref, *out_refs):
-    x, c = lax.axis_index("x"), lax.axis_index("c")
+def chip_sums_kernel(keep, hot_ref, own_ref, other_ref, out_ref):
     parts, half, cols = own_ref.shape
-    for k in (2, 1, 3, 0) if parts == 4 else range(parts):
-        start = pl.multiple_of((2 * lax.rem(x + k, parts) + c) * cols, LANES)
-        tokens = jnp.concatenate([own_ref[k], other_ref[:, pl.ds(start, cols)]], axis=0)
-        out_refs[k][...] = jnp.dot(hot_ref[...], tokens, preferred_element_type=jnp.float32).astype(jnp.bfloat16)
-
-
-def group_sums_kernel(rows_ref, *refs):
-    parts, out_ref = refs[:-1], refs[-1]
-    cols = parts[0].shape[1]
-    total = parts[0][...].astype(jnp.float32)
-    for ref in parts[1:]:
-        total += ref[...].astype(jnp.float32)
+    c, x, partner, later, across = chips(parts)
+    for k, chip in enumerate((x, later) if keep else (partner, across)):
+        tokens = jnp.concatenate([own_ref[2 * keep + k], other_ref[:, block(chip, c, cols)]], axis=0)
+        total = jnp.dot(hot_ref[...], tokens, preferred_element_type=jnp.float32)
+        out_ref[:, k * cols : (k + 1) * cols] = total.astype(out_ref.dtype)
+
+
+def pair_sums_kernel(kept_ref, arrived_ref, out_ref):
+    cols = out_ref.shape[1]
+    out_ref[...] = (kept_ref[:, cols:] + arrived_ref[:, cols:].astype(jnp.float32)).astype(jnp.bfloat16)
+
+
+def group_sums_kernel(rows_ref, kept_ref, arrived_ref, last_ref, out_ref):
+    cols = last_ref.shape[1]
+    total = kept_ref[:, :cols] + arrived_ref[:, :cols].astype(jnp.float32) + last_ref[...].astype(jnp.float32)
     out_ref[:, :cols] = total.astype(jnp.bfloat16)
     out_ref[:, cols:] = rows_ref[...]
 
@@ -131,25 +143,41 @@
         cost_estimate=pl.CostEstimate(flops=10**6, bytes_accessed=4 * 10**6, transcendentals=0),
         name="setup",
     )(token_ids.reshape(1, -1), slot_ids, grad_out)
-    sums = pl.pallas_call(
-        chip_sums_kernel,
-        out_shape=(jax.ShapeDtypeStruct((slots, cols), bf16),) * parts,
-        in_specs=[VMEM] * 3,
-        out_specs=(VMEM,) * parts,
+    def chip_sums(keep):
+        return pl.pallas_call(
+            lambda *refs: chip_sums_kernel(keep, *refs),
+            out_shape=jax.ShapeDtypeStruct((slots, 2 * cols), f32 if keep else bf16),
+            in_specs=[VMEM] * 3,
+            out_specs=VMEM,
+            compiler_params=limit,
+            cost_estimate=pl.CostEstimate(flops=8 * slots * half * cols, bytes_accessed=10**6, transcendentals=0),
+            name="chip_sums",
+        )(hot, own, other)
+
+    def exchange(values, first):
+        places = [(i, c) for i in range(parts) for c in range(2)]
+        to = [2 * (i ^ (1 if (c == 0) == first else parts - 1)) + c for i, c in places]
+        return lax.ppermute(values, ("x", "c"), list(enumerate(to)))
+
+    arrived = exchange(chip_sums(0), True)
+    kept = chip_sums(1)
+    outgoing = pl.pallas_call(
+        pair_sums_kernel,
+        out_shape=jax.ShapeDtypeStruct((slots, cols), bf16),
+        in_specs=[VMEM] * 2,
+        out_specs=VMEM,
         compiler_params=limit,
-        name="chip_sums",
-    )(hot, own, other)
-    arrived = [sums[0]]
-    for k in range(1, parts):
-        arrived.append(lax.ppermute(sums[k], "x", [(i, (i + k) % parts) for i in range(parts)]))
+        name="pair_sums",
+    )(kept, arrived)
+    last = exchange(outgoing, False)
     outgoing = pl.pallas_call(
         group_sums_kernel,
         out_shape=jax.ShapeDtypeStruct((slots, cols + LANES), bf16),
-        in_specs=[VMEM] * (parts + 1),
+        in_specs=[VMEM] * 4,
         out_specs=VMEM,
         compiler_params=limit,
         name="group_sums",
-    )(rows, *arrived)
+    )(rows, kept, arrived, last)
     outgoing = outgoing.reshape(slots // CAP, CAP, cols + LANES)
     slot_sums = lax.all_to_all(outgoing, "vocab", split_axis=0, concat_axis=0, tiled=True)
     slot_sums = slot_sums.reshape(slots, cols + LANES)

time: 79.8 us -> 76.9 us (0.964); the launches traced: 78.4 us -> 76.6 us
  starting transfers between devices: 18 us -> 16 us
  waiting for transfers between devices: 16.6 us -> 15.7 us
  blocking collectives: 36.9 us -> 37.8 us
    ppermute x3 -> x2, starting transfers between devices: 16.1 us -> 14.1 us  [exchange(): return lax.ppermute(values, ('x', 'c'), list(enumerate(to)))]
    ppermute x3 -> x2, waiting for transfers between devices: 15.9 us -> 14.9 us  [exchange(): return lax.ppermute(values, ('x', 'c'), list(enumerate(to)))]
    all_to_all x1, blocking collectives: 36.9 us -> 37.8 us  [per_device(): lax.all_to_all(outgoing, 'vocab', split_axis=0, concat_axis=0, tiled=True)]
  transfers between devices with their start and end apart: 4 -> 3, of which waited for: 3 -> 3; matrix products, arithmetic and copies ran while one was open for 0% -> 0% of each run, Pallas kernels for 0% -> 1%
where the time goes in v3:
time: 76.9 us; the launch traced here: 76.6 us
  blocking collectives  37.8 us (49%)
  starting transfers between devices  16 us (21%)
  waiting for transfers between devices  15.7 us (20%)
  local copies, waits for them, and re-layouts  3.17 us (4%)
  Pallas kernels  3.16 us (4%)
    all_to_all x1, blocking collectives, per_device(): lax.all_to_all(outgoing, 'vocab', split_axis=0, concat_axis=0, tiled=True)  37.8 us
    ppermute x2, waiting for transfers between devices, exchange(): return lax.ppermute(values, ('x', 'c'), list(enumerate(to)))  14.9 us
    ppermute x2, starting transfers between devices, exchange(): return lax.ppermute(values, ('x', 'c'), list(enumerate(to)))  14.1 us
    unnamed x12, local copies, waits for them, and re-layouts  2.88 us
    ppermute x1, starting transfers between devices, per_device(): other = lax.ppermute(grad_out, 'c', [(0, 1), (1, 0)])  1.92 us
    pallas_call x1, Pallas kernels, per_device(): pl.pallas_call(update_kernel, out_shape=(jax.ShapeDtypeStruct(param.shape...  1.88 us
  transfers between devices with their start and end apart: 3, of which 3 were waited for; matrix products, arithmetic and copies ran while one was open for 0% of the time, Pallas kernels for 1%

profile of v3, /device:TPU:6, one launch (start us, length us, event | category | flops | bytes accessed | tf_op | source)
XLA Modules:
  0.0 76.6 jit_solution(18134994665144528081)
XLA Ops:
  0.6 1.9 %collective-permute-start = (bf16[128,7168]{1,0:T(8,128)(2,1)}, bf16[128,7168]{1,0:T(8,128)(2,1)S(1)}, u32[]{:S(2)}, u32[]{:S(2)}) collective-permute-start(bf16[128,7168]{1,0:T(8,128)(2,1)} %refs_2_.1), channel_id=1, source_target_pairs={{0,1},{1,0},{2,3},{3,2},{4,5},{5,4},{6,7},{7,6},{8,9},{9,8},{10,11... | collective-permute-start | bytes 5505032 | tf_op jit(solution)/shard_map/ppermute | solution.py:127
  2.6 0.0 copy-start
  2.6 1.5 %copy-done = bf16[128,7168]{1,0:T(8,128)(2,1)S(1)} copy-done((bf16[128,7168]{1,0:T(8,128)(2,1)S(1)}, bf16[128,7168]{1,0:T(8,128)(2,1)}, u32[]{:S(2)}) %copy-start) | copy-done | bytes 1835032
  4.1 0.0 copy-start.4
  4.1 0.7 copy-done.4
  4.7 0.0 copy-start.5
  4.7 0.7 copy-done.5
  5.4 0.3 setup.1
  5.8 0.7 collective-permute-done.refs_2_
  6.5 0.4 chip_sums.3
  6.9 2.7 %collective-permute-start.1 = (bf16[192,1792]{1,0:T(8,128)(2,1)S(1)}, bf16[192,1792]{1,0:T(8,128)(2,1)S(1)}, u32[]{:S(2)}, u32[]{:S(2)}) collective-permute-start(bf16[192,1792]{1,0:T(8,128)(2,1)S(1)} %chip_sums.3), channel_id=1, source_target_pairs={{0,2},{1,7},{2,0},{3,5},{4,6},{5,3},{6,4},{7,1},{8,10},{9,15},{10,... | collective-permute-start | bytes 2064392 | tf_op jit(solution)/shard_map/ppermute | solution.py:160
  9.7 0.4 chip_sums.2.kept_ref
  10.0 9.7 %collective-permute-done.1.arrived_ref = bf16[192,1792]{1,0:T(8,128)(2,1)S(1)} collective-permute-done((bf16[192,1792]{1,0:T(8,128)(2,1)S(1)}, bf16[192,1792]{1,0:T(8,128)(2,1)S(1)}, u32[]{:S(2)}, u32[]{:S(2)}) %collective-permute-start.1) | collective-permute-done | bytes 688160 | tf_op jit(solution)/shard_map/ppermute | solution.py:160
  19.7 0.1 pair_sums.1
  19.8 11.4 %collective-permute-start.2 = (bf16[192,896]{1,0:T(8,128)(2,1)S(1)}, bf16[192,896]{1,0:T(8,128)(2,1)S(1)}, u32[]{:S(2)}, u32[]{:S(2)}) collective-permute-start(bf16[192,896]{1,0:T(8,128)(2,1)S(1)} %pair_sums.1), channel_id=1, source_target_pairs={{0,6},{1,3},{2,4},{3,1},{4,2},{5,7},{6,0},{7,5},{8,14},{9,11},{10,... | collective-permute-start | bytes 1032200 | tf_op jit(solution)/shard_map/ppermute | solution.py:160
  31.2 5.2 %collective-permute-done.2.last_ref = bf16[192,896]{1,0:T(8,128)(2,1)S(1)} collective-permute-done((bf16[192,896]{1,0:T(8,128)(2,1)S(1)}, bf16[192,896]{1,0:T(8,128)(2,1)S(1)}, u32[]{:S(2)}, u32[]{:S(2)}) %collective-permute-start.2) | collective-permute-done | bytes 344096 | tf_op jit(solution)/shard_map/ppermute | solution.py:160
  36.4 0.1 group_sums.1
  36.5 0.0 copy-start.1
  36.5 0.0 copy-start.2
  36.6 0.0 copy-start.3
  36.6 0.1 reshape.16
  36.7 37.8 %all_to_all.5 = bf16[96,2,1024]{2,1,0:T(2,128)(2,1)S(1)} all-to-all(bf16[96,2,1024]{2,1,0:T(2,128)(2,1)S(1)} %reshape.16), channel_id=1, replica_groups=mesh['vocab'=96,'x'=4,'c'=2] {'vocab'}, dimensions={0} | all-to-all | bytes 786432 | tf_op jit(solution)/shard_map/all_to_all | solution.py:182
  74.5 0.1 reshape.17.sums_ref
  74.7 0.0 copy-done.1
  74.7 0.0 copy-done.2
  74.7 0.0 copy-done.3
  74.7 1.9 %update.1 = (f32[192,896]{1,0:T(8,128)}, bf16[192,896]{1,0:T(8,128)(2,1)}, bf16[192,896]{1,0:T(8,128)(2,1)}) custom-call(bf16[192,1024]{1,0:T(8,128)(2,1)S(1)} %reshape.17.sums_ref, f32[192,896]{1,0:T(8,128)S(1)} %copy-done.1, bf16[192,896]{1,0:T(8,128)(2,1)S(1)} %copy-done.2, bf16[192,896]{1,0:T(8,128)(2,1)S(1)} %copy-done.3), custom_call_target="tpu_custom_call" | custom-call | tf_op jit(solution)/shard_map/update/pallas_call | solution.py:186
Async XLA Ops:
  0.6 5.9 %collective-permute-start = (bf16[128,7168]{1,0:T(8,128)(2,1)}, bf16[128,7168]{1,0:T(8,128)(2,1)S(1)}, u32[]{:S(2)}, u32[]{:S(2)}) collective-permute-start(bf16[128,7168]{1,0:T(8,128)(2,1)} %refs_2_.1), channel_id=1, source_target_pairs={{0,1},{1,0},{2,3},{3,2},{4,5},{5,4},{6,7},{7,6},{8,9},{9,8},{10,11... | collective-permute-start | bytes 5505032 | tf_op jit(solution)/shard_map/ppermute | solution.py:127
  2.6 1.5 %copy-start = (bf16[128,7168]{1,0:T(8,128)(2,1)S(1)}, bf16[128,7168]{1,0:T(8,128)(2,1)}, u32[]{:S(2)}) copy-start(bf16[128,7168]{1,0:T(8,128)(2,1)} %refs_2_.1) | copy-start | bytes 5505028
  4.1 0.7 copy-start.4
  4.7 0.7 copy-start.5
  6.9 12.8 %collective-permute-start.1 = (bf16[192,1792]{1,0:T(8,128)(2,1)S(1)}, bf16[192,1792]{1,0:T(8,128)(2,1)S(1)}, u32[]{:S(2)}, u32[]{:S(2)}) collective-permute-start(bf16[192,1792]{1,0:T(8,128)(2,1)S(1)} %chip_sums.3), channel_id=1, source_target_pairs={{0,2},{1,7},{2,0},{3,5},{4,6},{5,3},{6,4},{7,1},{8,10},{9,15},{10,... | collective-permute-start | bytes 2064392 | tf_op jit(solution)/shard_map/ppermute | solution.py:160
  19.8 16.6 %collective-permute-start.2 = (bf16[192,896]{1,0:T(8,128)(2,1)S(1)}, bf16[192,896]{1,0:T(8,128)(2,1)S(1)}, u32[]{:S(2)}, u32[]{:S(2)}) collective-permute-start(bf16[192,896]{1,0:T(8,128)(2,1)S(1)} %pair_sums.1), channel_id=1, source_target_pairs={{0,6},{1,3},{2,4},{3,1},{4,2},{5,7},{6,0},{7,5},{8,14},{9,11},{10,... | collective-permute-start | bytes 1032200 | tf_op jit(solution)/shard_map/ppermute | solution.py:160
  36.5 38.2 %copy-start.1 = (f32[192,896]{1,0:T(8,128)S(1)}, f32[192,896]{1,0:T(8,128)}, u32[]{:S(2)}) copy-start(f32[192,896]{1,0:T(8,128)} %param_ref.1) | copy-start | bytes 2064388
  36.5 38.2 %copy-start.2 = (bf16[192,896]{1,0:T(8,128)(2,1)S(1)}, bf16[192,896]{1,0:T(8,128)(2,1)}, u32[]{:S(2)}) copy-start(bf16[192,896]{1,0:T(8,128)(2,1)} %first_ref.1) | copy-start | bytes 1032196
  36.6 38.2 %copy-start.3 = (bf16[192,896]{1,0:T(8,128)(2,1)S(1)}, bf16[192,896]{1,0:T(8,128)(2,1)}, u32[]{:S(2)}) copy-start(bf16[192,896]{1,0:T(8,128)(2,1)} %second_ref.1) | copy-start | bytes 1032196

commit v4 on v3

--- a/solution.py
+++ b/solution.py
@@ -43,7 +43,7 @@
     ]
     large = [
         pltpu.make_async_copy(grad_ref.at[:, block(chip, c, cols)], own_ref.at[k], sems.at[k])
-        for k, chip in enumerate((partner, across, x, later))
+        for k, chip in enumerate((across, partner, x, later))
     ]
     for copy in small + large:
         copy.start()
@@ -63,23 +63,23 @@
         copy.wait()
 
 
-def chip_sums_kernel(keep, hot_ref, own_ref, other_ref, out_ref):
+def chip_sums_kernel(which, hot_ref, own_ref, other_ref, *out_refs):
     parts, half, cols = own_ref.shape
     c, x, partner, later, across = chips(parts)
-    for k, chip in enumerate((x, later) if keep else (partner, across)):
-        tokens = jnp.concatenate([own_ref[2 * keep + k], other_ref[:, block(chip, c, cols)]], axis=0)
+    for k, out_ref in zip(which, out_refs):
+        chip = (across, partner, x, later)[k]
+        tokens = jnp.concatenate([own_ref[k], other_ref[:, block(chip, c, cols)]], axis=0)
         total = jnp.dot(hot_ref[...], tokens, preferred_element_type=jnp.float32)
-        out_ref[:, k * cols : (k + 1) * cols] = total.astype(out_ref.dtype)
+        out_ref[...] = total.astype(out_ref.dtype)
 
 
 def pair_sums_kernel(kept_ref, arrived_ref, out_ref):
-    cols = out_ref.shape[1]
-    out_ref[...] = (kept_ref[:, cols:] + arrived_ref[:, cols:].astype(jnp.float32)).astype(jnp.bfloat16)
+    out_ref[...] = (kept_ref[...] + arrived_ref[...].astype(jnp.float32)).astype(jnp.bfloat16)
 
 
 def group_sums_kernel(rows_ref, kept_ref, arrived_ref, last_ref, out_ref):
     cols = last_ref.shape[1]
-    total = kept_ref[:, :cols] + arrived_ref[:, :cols].astype(jnp.float32) + last_ref[...].astype(jnp.float32)
+    total = kept_ref[...] + arrived_ref[...].astype(jnp.float32) + last_ref[...].astype(jnp.float32)
     out_ref[:, :cols] = total.astype(jnp.bfloat16)
     out_ref[:, cols:] = rows_ref[...]
 
@@ -143,12 +143,13 @@
         cost_estimate=pl.CostEstimate(flops=10**6, bytes_accessed=4 * 10**6, transcendentals=0),
         name="setup",
     )(token_ids.reshape(1, -1), slot_ids, grad_out)
-    def chip_sums(keep):
+    def chip_sums(which, dtype):
+        outs = tuple(jax.ShapeDtypeStruct((slots, cols), dtype) for k in which)
         return pl.pallas_call(
-            lambda *refs: chip_sums_kernel(keep, *refs),
-            out_shape=jax.ShapeDtypeStruct((slots, 2 * cols), f32 if keep else bf16),
+            lambda *refs: chip_sums_kernel(which, *refs),
+            out_shape=outs,
             in_specs=[VMEM] * 3,
-            out_specs=VMEM,
+            out_specs=(VMEM,) * len(which),
             compiler_params=limit,
             cost_estimate=pl.CostEstimate(flops=8 * slots * half * cols, bytes_accessed=10**6, transcendentals=0),
             name="chip_sums",
@@ -159,8 +160,9 @@
         to = [2 * (i ^ (1 if (c == 0) == first else parts - 1)) + c for i, c in places]
         return lax.ppermute(values, ("x", "c"), list(enumerate(to)))
 
-    arrived = exchange(chip_sums(0), True)
-    kept = chip_sums(1)
+    first = exchange(*chip_sums((0,), bf16), True)
+    second = exchange(*chip_sums((1,), bf16), True)
+    kept, passing = chip_sums((2, 3), f32)
     outgoing = pl.pallas_call(
         pair_sums_kernel,
         out_shape=jax.ShapeDtypeStruct((slots, cols), bf16),
@@ -168,7 +170,7 @@
         out_specs=VMEM,
         compiler_params=limit,
         name="pair_sums",
-    )(kept, arrived)
+    )(passing, first)
     last = exchange(outgoing, False)
     outgoing = pl.pallas_call(
         group_sums_kernel,
@@ -177,7 +179,7 @@
         out_specs=VMEM,
         compiler_params=limit,
         name="group_sums",
-    )(rows, kept, arrived, last)
+    )(rows, kept, second, last)
     outgoing = outgoing.reshape(slots // CAP, CAP, cols + LANES)
     slot_sums = lax.all_to_all(outgoing, "vocab", split_axis=0, concat_axis=0, tiled=True)
     slot_sums = slot_sums.reshape(slots, cols + LANES)

time: 76.9 us -> 73.1 us (0.951)
  waiting for transfers between devices: 15.7 us -> 8.55 us
  starting transfers between devices: 16 us -> 19.2 us
    ppermute x2 -> x3, waiting for transfers between devices: 14.9 us -> 7.81 us  [exchange(): return lax.ppermute(values, ('x', 'c'), list(enumerate(to)))]
    ppermute x2 -> x3, starting transfers between devices: 14.1 us -> 17.2 us  [exchange(): return lax.ppermute(values, ('x', 'c'), list(enumerate(to)))]
  transfers between devices with their start and end apart: 3 -> 4, of which waited for: 3 -> 3; matrix products, arithmetic and copies ran while one was open for 0% -> 0% of each run, Pallas kernels for 1% -> 2%
where the time goes in v4:
time: 73.1 us; the launch traced here: 72.8 us
  blocking collectives  37.8 us (52%)
  starting transfers between devices  19.2 us (26%)
  waiting for transfers between devices  8.55 us (12%)
  Pallas kernels  3.37 us (5%)
  local copies, waits for them, and re-layouts  3.17 us (4%)
  between operations  0.76 us (1%)
    all_to_all x1, blocking collectives, per_device(): lax.all_to_all(outgoing, 'vocab', split_axis=0, concat_axis=0, tiled=True)  37.8 us
    ppermute x3, starting transfers between devices, exchange(): return lax.ppermute(values, ('x', 'c'), list(enumerate(to)))  17.2 us
    ppermute x3, waiting for transfers between devices, exchange(): return lax.ppermute(values, ('x', 'c'), list(enumerate(to)))  7.81 us
    unnamed x12, local copies, waits for them, and re-layouts  2.87 us
    ppermute x1, starting transfers between devices, per_device(): other = lax.ppermute(grad_out, 'c', [(0, 1), (1, 0)])  1.92 us
    pallas_call x1, Pallas kernels, per_device(): pl.pallas_call(update_kernel, out_shape=(jax.ShapeDtypeStruct(param.shape...  1.88 us
  transfers between devices with their start and end apart: 4, of which 3 were waited for; matrix products, arithmetic and copies ran while one was open for 0% of the time, Pallas kernels for 2%

profile of v4, /device:TPU:6, one launch (start us, length us, event | category | flops | bytes accessed | tf_op | source)
XLA Modules:
  0.0 72.8 jit_solution(4581450469932982806)
XLA Ops:
  0.6 1.9 %collective-permute-start = (bf16[128,7168]{1,0:T(8,128)(2,1)}, bf16[128,7168]{1,0:T(8,128)(2,1)S(1)}, u32[]{:S(2)}, u32[]{:S(2)}) collective-permute-start(bf16[128,7168]{1,0:T(8,128)(2,1)} %refs_2_.1), channel_id=1, source_target_pairs={{0,1},{1,0},{2,3},{3,2},{4,5},{5,4},{6,7},{7,6},{8,9},{9,8},{10,11... | collective-permute-start | bytes 5505032 | tf_op jit(solution)/shard_map/ppermute | solution.py:127
  2.6 0.0 copy-start
  2.6 1.5 %copy-done = bf16[128,7168]{1,0:T(8,128)(2,1)S(1)} copy-done((bf16[128,7168]{1,0:T(8,128)(2,1)S(1)}, bf16[128,7168]{1,0:T(8,128)(2,1)}, u32[]{:S(2)}) %copy-start) | copy-done | bytes 1835032
  4.1 0.0 copy-start.4
  4.1 0.7 copy-done.4
  4.7 0.0 copy-start.5
  4.7 0.7 copy-done.5
  5.4 0.3 setup.1
  5.8 0.7 %collective-permute-done.refs_2_ = bf16[128,7168]{1,0:T(8,128)(2,1)S(1)} collective-permute-done((bf16[128,7168]{1,0:T(8,128)(2,1)}, bf16[128,7168]{1,0:T(8,128)(2,1)S(1)}, u32[]{:S(2)}, u32[]{:S(2)}) %collective-permute-start) | collective-permute-done | bytes 1835040 | tf_op jit(solution)/shard_map/ppermute | solution.py:127
  6.5 0.3 chip_sums.5
  6.8 2.7 %collective-permute-start.2 = (bf16[192,896]{1,0:T(8,128)(2,1)S(1)}, bf16[192,896]{1,0:T(8,128)(2,1)S(1)}, u32[]{:S(2)}, u32[]{:S(2)}) collective-permute-start(bf16[192,896]{1,0:T(8,128)(2,1)S(1)} %chip_sums.5), channel_id=1, source_target_pairs={{0,2},{1,7},{2,0},{3,5},{4,6},{5,3},{6,4},{7,1},{8,10},{9,15},{10,... | collective-permute-start | bytes 1032200 | tf_op jit(solution)/shard_map/ppermute | solution.py:161
  9.5 0.3 chip_sums.4
  9.8 3.1 %collective-permute-start.1 = (bf16[192,896]{1,0:T(8,128)(2,1)S(1)}, bf16[192,896]{1,0:T(8,128)(2,1)S(1)}, u32[]{:S(2)}, u32[]{:S(2)}) collective-permute-start(bf16[192,896]{1,0:T(8,128)(2,1)S(1)} %chip_sums.4), channel_id=1, source_target_pairs={{0,2},{1,7},{2,0},{3,5},{4,6},{5,3},{6,4},{7,1},{8,10},{9,15},{10,... | collective-permute-start | bytes 1032200 | tf_op jit(solution)/shard_map/ppermute | solution.py:161
  12.9 0.4 chip_sums.3
  13.3 2.6 %collective-permute-done.2.arrived_ref = bf16[192,896]{1,0:T(8,128)(2,1)S(1)} collective-permute-done((bf16[192,896]{1,0:T(8,128)(2,1)S(1)}, bf16[192,896]{1,0:T(8,128)(2,1)S(1)}, u32[]{:S(2)}, u32[]{:S(2)}) %collective-permute-start.2) | collective-permute-done | bytes 344096 | tf_op jit(solution)/shard_map/ppermute | solution.py:161
  15.9 0.1 pair_sums.1
  16.0 11.4 %collective-permute-start.3 = (bf16[192,896]{1,0:T(8,128)(2,1)S(1)}, bf16[192,896]{1,0:T(8,128)(2,1)S(1)}, u32[]{:S(2)}, u32[]{:S(2)}) collective-permute-start(bf16[192,896]{1,0:T(8,128)(2,1)S(1)} %pair_sums.1), channel_id=1, source_target_pairs={{0,6},{1,3},{2,4},{3,1},{4,2},{5,7},{6,0},{7,5},{8,14},{9,11},{10,... | collective-permute-start | bytes 1032200 | tf_op jit(solution)/shard_map/ppermute | solution.py:161
  27.4 0.0 collective-permute-done.1.arrived_ref
  27.4 5.2 %collective-permute-done.3.last_ref = bf16[192,896]{1,0:T(8,128)(2,1)S(1)} collective-permute-done((bf16[192,896]{1,0:T(8,128)(2,1)S(1)}, bf16[192,896]{1,0:T(8,128)(2,1)S(1)}, u32[]{:S(2)}, u32[]{:S(2)}) %collective-permute-start.3) | collective-permute-done | bytes 344096 | tf_op jit(solution)/shard_map/ppermute | solution.py:161
  32.6 0.0 copy-start.1
  32.6 0.0 copy-start.2
  32.7 0.0 copy-start.3
  32.7 0.1 group_sums.1
  32.8 0.1 reshape.16
  32.9 37.8 %all_to_all.5 = bf16[96,2,1024]{2,1,0:T(2,128)(2,1)S(1)} all-to-all(bf16[96,2,1024]{2,1,0:T(2,128)(2,1)S(1)} %reshape.16), channel_id=1, replica_groups=mesh['vocab'=96,'x'=4,'c'=2] {'vocab'}, dimensions={0} | all-to-all | bytes 786432 | tf_op jit(solution)/shard_map/all_to_all | solution.py:184
  70.8 0.1 reshape.17.sums_ref
  70.9 0.0 copy-done.1
  70.9 0.0 copy-done.2
  70.9 0.0 copy-done.3
  70.9 1.9 %update.1 = (f32[192,896]{1,0:T(8,128)}, bf16[192,896]{1,0:T(8,128)(2,1)}, bf16[192,896]{1,0:T(8,128)(2,1)}) custom-call(bf16[192,1024]{1,0:T(8,128)(2,1)S(1)} %reshape.17.sums_ref, f32[192,896]{1,0:T(8,128)S(1)} %copy-done.1, bf16[192,896]{1,0:T(8,128)(2,1)S(1)} %copy-done.2, bf16[192,896]{1,0:T(8,128)(2,1)S(1)} %copy-done.3), custom_call_target="tpu_custom_call" | custom-call | tf_op jit(solution)/shard_map/update/pallas_call | solution.py:188
Async XLA Ops:
  0.6 5.9 %collective-permute-start = (bf16[128,7168]{1,0:T(8,128)(2,1)}, bf16[128,7168]{1,0:T(8,128)(2,1)S(1)}, u32[]{:S(2)}, u32[]{:S(2)}) collective-permute-start(bf16[128,7168]{1,0:T(8,128)(2,1)} %refs_2_.1), channel_id=1, source_target_pairs={{0,1},{1,0},{2,3},{3,2},{4,5},{5,4},{6,7},{7,6},{8,9},{9,8},{10,11... | collective-permute-start | bytes 5505032 | tf_op jit(solution)/shard_map/ppermute | solution.py:127
  2.6 1.5 %copy-start = (bf16[128,7168]{1,0:T(8,128)(2,1)S(1)}, bf16[128,7168]{1,0:T(8,128)(2,1)}, u32[]{:S(2)}) copy-start(bf16[128,7168]{1,0:T(8,128)(2,1)} %refs_2_.1) | copy-start | bytes 5505028
  4.1 0.7 copy-start.4
  4.7 0.7 copy-start.5
  6.8 9.1 %collective-permute-start.2 = (bf16[192,896]{1,0:T(8,128)(2,1)S(1)}, bf16[192,896]{1,0:T(8,128)(2,1)S(1)}, u32[]{:S(2)}, u32[]{:S(2)}) collective-permute-start(bf16[192,896]{1,0:T(8,128)(2,1)S(1)} %chip_sums.5), channel_id=1, source_target_pairs={{0,2},{1,7},{2,0},{3,5},{4,6},{5,3},{6,4},{7,1},{8,10},{9,15},{10,... | collective-permute-start | bytes 1032200 | tf_op jit(solution)/shard_map/ppermute | solution.py:161
  9.8 17.6 %collective-permute-start.1 = (bf16[192,896]{1,0:T(8,128)(2,1)S(1)}, bf16[192,896]{1,0:T(8,128)(2,1)S(1)}, u32[]{:S(2)}, u32[]{:S(2)}) collective-permute-start(bf16[192,896]{1,0:T(8,128)(2,1)S(1)} %chip_sums.4), channel_id=1, source_target_pairs={{0,2},{1,7},{2,0},{3,5},{4,6},{5,3},{6,4},{7,1},{8,10},{9,15},{10,... | collective-permute-start | bytes 1032200 | tf_op jit(solution)/shard_map/ppermute | solution.py:161
  16.0 16.6 %collective-permute-start.3 = (bf16[192,896]{1,0:T(8,128)(2,1)S(1)}, bf16[192,896]{1,0:T(8,128)(2,1)S(1)}, u32[]{:S(2)}, u32[]{:S(2)}) collective-permute-start(bf16[192,896]{1,0:T(8,128)(2,1)S(1)} %pair_sums.1), channel_id=1, source_target_pairs={{0,6},{1,3},{2,4},{3,1},{4,2},{5,7},{6,0},{7,5},{8,14},{9,11},{10,... | collective-permute-start | bytes 1032200 | tf_op jit(solution)/shard_map/ppermute | solution.py:161
  32.6 38.3 %copy-start.1 = (f32[192,896]{1,0:T(8,128)S(1)}, f32[192,896]{1,0:T(8,128)}, u32[]{:S(2)}) copy-start(f32[192,896]{1,0:T(8,128)} %param_ref.1) | copy-start | bytes 2064388
  32.6 38.3 %copy-start.2 = (bf16[192,896]{1,0:T(8,128)(2,1)S(1)}, bf16[192,896]{1,0:T(8,128)(2,1)}, u32[]{:S(2)}) copy-start(bf16[192,896]{1,0:T(8,128)(2,1)} %first_ref.1) | copy-start | bytes 1032196
  32.7 38.3 %copy-start.3 = (bf16[192,896]{1,0:T(8,128)(2,1)S(1)}, bf16[192,896]{1,0:T(8,128)(2,1)}, u32[]{:S(2)}) copy-start(bf16[192,896]{1,0:T(8,128)(2,1)} %second_ref.1) | copy-start | bytes 1032196

commit v5 on v4

--- a/solution.py
+++ b/solution.py
@@ -13,9 +13,14 @@
 CORRECT_ONE = 1.0 - 0.9**10
 CORRECT_TWO = 1.0 - 0.95**10
 CAP = 2
+SPREAD = (35, 30)
 LANES = 128
 VMEM = pl.BlockSpec(memory_space=pltpu.VMEM)
 HBM = pl.BlockSpec(memory_space=pltpu.HBM)
+
+
+def member(place, groups):
+    return place * (SPREAD[0] + SPREAD[1] * place) % groups
 
 
 def one_hot(mask):
@@ -49,14 +54,15 @@
         copy.start()
     for copy in small:
         copy.wait()
-    row = lax.broadcasted_iota(jnp.int32, (slots, slots), 0)
+    row = lax.broadcasted_iota(jnp.int32, (slots, LANES), 0)
+    owner = member(row // CAP, slots // CAP)
+    source = jnp.broadcast_to((CAP * owner + row % CAP)[:, :1], (slots, slots))
     lane = lax.broadcasted_iota(jnp.int32, (slots, slots), 1)
     wide = jnp.broadcast_to(slot_row[...], (slots, slots))
-    column = jnp.sum(jnp.where(lane == row, wide, 0), axis=1, keepdims=True)
+    column = jnp.sum(jnp.where(lane == source, wide, 0), axis=1, keepdims=True)
     low, high = tokens[:, :half], tokens[:, half:]
     hot_ref[:, :half] = one_hot(column == jnp.where(c == 0, low, high))
     hot_ref[:, half:] = one_hot(column == jnp.where(c == 0, high, low))
-    owner = lax.broadcasted_iota(jnp.int32, (slots, LANES), 0) // CAP
     local = jnp.where(column < 0, -1, column - owner * block_rows)
     rows_ref[...] = local.astype(jnp.float32).astype(jnp.bfloat16)
     for copy in large:
@@ -87,27 +93,25 @@
 def update_kernel(sums_ref, param_ref, first_ref, second_ref, *refs):
     outs, (param_buf, first_buf, second_buf, sems) = refs[:3], refs[3:]
     block_rows, cols = param_ref.shape
-    names = sums_ref[:, cols:].astype(jnp.int32)
-    row = lax.broadcasted_iota(jnp.int32, names.shape, 1)
+    names = sums_ref[:, cols:].astype(jnp.float32).T
+    row = lax.broadcasted_iota(jnp.int32, names.shape, 0).astype(jnp.float32)
     pieces = [one_hot(names == row + start) for start in range(0, block_rows, LANES)]
-    selector = jnp.concatenate(pieces, axis=1)
+    selector = jnp.concatenate(pieces, axis=0)[:block_rows]
     copies = []
     step = 2 * LANES if cols % (2 * LANES) == 0 else LANES
     step = cols // 7 * 2 if cols % (7 * LANES) == 0 else step
     edges = list(range(0, cols, step)) + [cols]
     for i, (lo, hi) in enumerate(zip(edges[:-1], edges[1:])):
-        table_grad = lax.dot_general(
-            selector, sums_ref[:, lo:hi], (((0,), (0,)), ((), ())), preferred_element_type=jnp.float32
-        )[:block_rows]
+        table_grad = jnp.dot(selector, sums_ref[:, lo:hi], preferred_element_type=jnp.float32)
         first = BETA_ONE * first_ref[:, lo:hi].astype(jnp.float32) + (1.0 - BETA_ONE) * table_grad
         second = BETA_TWO * second_ref[:, lo:hi].astype(jnp.float32) + (1.0 - BETA_TWO) * table_grad * table_grad
         first, second = first.astype(jnp.bfloat16), second.astype(jnp.bfloat16)
         first_buf[:, lo:hi] = first
         second_buf[:, lo:hi] = second
-        scale = jnp.sqrt(second.astype(jnp.float32) * (1.0 / CORRECT_TWO)) + EPSILON
-        change = first.astype(jnp.float32) * (1.0 / CORRECT_ONE) / scale
-        old = param_ref[:, lo:hi]
-        param_buf[:, lo:hi] = old - LEARN_RATE * (change + WEIGHT_DECAY * old)
+        square = second.astype(jnp.float32) * (1.0 / CORRECT_TWO)
+        scale = pl.reciprocal(square * lax.rsqrt(square) + EPSILON)
+        change = first.astype(jnp.float32) * (LEARN_RATE / CORRECT_ONE) * scale
+        param_buf[:, lo:hi] = param_ref[:, lo:hi] * (1.0 - LEARN_RATE * WEIGHT_DECAY) - change
         for j, (buf, out) in enumerate(zip((param_buf, first_buf, second_buf), outs)):
             copy = pltpu.make_async_copy(buf.at[:, pl.ds(lo, hi - lo)], out.at[:, pl.ds(lo, hi - lo)], sems.at[i, j])
             copy.start()
@@ -181,7 +185,11 @@
         name="group_sums",
     )(rows, kept, second, last)
     outgoing = outgoing.reshape(slots // CAP, CAP, cols + LANES)
-    slot_sums = lax.all_to_all(outgoing, "vocab", split_axis=0, concat_axis=0, tiled=True)
+    groups = slots // CAP
+    order = [member(place, groups) for place in range(groups)]
+    slot_sums = lax.all_to_all(
+        outgoing, "vocab", split_axis=0, concat_axis=0, axis_index_groups=[order], tiled=True
+    )
     slot_sums = slot_sums.reshape(slots, cols + LANES)
     chunks = 8
     return tuple(

time: 73.1 us -> 71 us (0.971)
  blocking collectives: 37.8 us -> 35.2 us
    all_to_all x1, blocking collectives: 37.8 us -> 35.2 us  [per_device(): lax.all_to_all(outgoing, 'vocab', split_axis=0, concat_axis=0, axis_index...]
where the time goes in v5:
time: 71 us; the launch traced here: 70.1 us
  blocking collectives  35.2 us (50%)
  starting transfers between devices  19.2 us (27%)
  waiting for transfers between devices  8.47 us (12%)
  Pallas kernels  3.31 us (5%)
  local copies, waits for them, and re-layouts  3.17 us (4%)
  between operations  0.76 us (1%)
    all_to_all x1, blocking collectives, per_device(): lax.all_to_all(outgoing, 'vocab', split_axis=0, concat_axis=0, axis_index...  35.2 us
    ppermute x3, starting transfers between devices, exchange(): return lax.ppermute(values, ('x', 'c'), list(enumerate(to)))  17.2 us
    ppermute x3, waiting for transfers between devices, exchange(): return lax.ppermute(values, ('x', 'c'), list(enumerate(to)))  7.81 us
    unnamed x12, local copies, waits for them, and re-layouts  2.87 us
    ppermute x1, starting transfers between devices, per_device(): other = lax.ppermute(grad_out, 'c', [(0, 1), (1, 0)])  1.92 us
    pallas_call x1, Pallas kernels, per_device(): pl.pallas_call(update_kernel, out_shape=(jax.ShapeDtypeStruct(param.shape...  1.74 us
  transfers between devices with their start and end apart: 4, of which 3 were waited for; matrix products, arithmetic and copies ran while one was open for 0% of the time, Pallas kernels for 2%

profile of v5, /device:TPU:6, one launch (start us, length us, event | category | flops | bytes accessed | tf_op | source)
XLA Modules:
  0.0 70.1 jit_solution(18063954466286454338)
XLA Ops:
  0.6 1.9 %collective-permute-start = (bf16[128,7168]{1,0:T(8,128)(2,1)}, bf16[128,7168]{1,0:T(8,128)(2,1)S(1)}, u32[]{:S(2)}, u32[]{:S(2)}) collective-permute-start(bf16[128,7168]{1,0:T(8,128)(2,1)} %refs_2_.1), channel_id=1, source_target_pairs={{0,1},{1,0},{2,3},{3,2},{4,5},{5,4},{6,7},{7,6},{8,9},{9,8},{10,11... | collective-permute-start | bytes 5505032 | tf_op jit(solution)/shard_map/ppermute | solution.py:131
  2.6 0.0 copy-start
  2.6 1.5 %copy-done = bf16[128,7168]{1,0:T(8,128)(2,1)S(1)} copy-done((bf16[128,7168]{1,0:T(8,128)(2,1)S(1)}, bf16[128,7168]{1,0:T(8,128)(2,1)}, u32[]{:S(2)}) %copy-start) | copy-done | bytes 1835032
  4.1 0.0 copy-start.4
  4.1 0.7 copy-done.4
  4.7 0.0 copy-start.5
  4.7 0.7 copy-done.5
  5.4 0.4 setup.1
  5.9 0.7 collective-permute-done.refs_2_
  6.5 0.3 chip_sums.5
  6.8 2.7 %collective-permute-start.2 = (bf16[192,896]{1,0:T(8,128)(2,1)S(1)}, bf16[192,896]{1,0:T(8,128)(2,1)S(1)}, u32[]{:S(2)}, u32[]{:S(2)}) collective-permute-start(bf16[192,896]{1,0:T(8,128)(2,1)S(1)} %chip_sums.5), channel_id=1, source_target_pairs={{0,2},{1,7},{2,0},{3,5},{4,6},{5,3},{6,4},{7,1},{8,10},{9,15},{10,... | collective-permute-start | bytes 1032200 | tf_op jit(solution)/shard_map/ppermute | solution.py:165
  9.5 0.3 chip_sums.4
  9.8 3.1 %collective-permute-start.1 = (bf16[192,896]{1,0:T(8,128)(2,1)S(1)}, bf16[192,896]{1,0:T(8,128)(2,1)S(1)}, u32[]{:S(2)}, u32[]{:S(2)}) collective-permute-start(bf16[192,896]{1,0:T(8,128)(2,1)S(1)} %chip_sums.4), channel_id=1, source_target_pairs={{0,2},{1,7},{2,0},{3,5},{4,6},{5,3},{6,4},{7,1},{8,10},{9,15},{10,... | collective-permute-start | bytes 1032200 | tf_op jit(solution)/shard_map/ppermute | solution.py:165
  12.9 0.4 chip_sums.3
  13.3 2.6 %collective-permute-done.2.arrived_ref = bf16[192,896]{1,0:T(8,128)(2,1)S(1)} collective-permute-done((bf16[192,896]{1,0:T(8,128)(2,1)S(1)}, bf16[192,896]{1,0:T(8,128)(2,1)S(1)}, u32[]{:S(2)}, u32[]{:S(2)}) %collective-permute-start.2) | collective-permute-done | bytes 344096 | tf_op jit(solution)/shard_map/ppermute | solution.py:165
  15.9 0.1 pair_sums.1
  16.0 11.4 %collective-permute-start.3 = (bf16[192,896]{1,0:T(8,128)(2,1)S(1)}, bf16[192,896]{1,0:T(8,128)(2,1)S(1)}, u32[]{:S(2)}, u32[]{:S(2)}) collective-permute-start(bf16[192,896]{1,0:T(8,128)(2,1)S(1)} %pair_sums.1), channel_id=1, source_target_pairs={{0,6},{1,3},{2,4},{3,1},{4,2},{5,7},{6,0},{7,5},{8,14},{9,11},{10,... | collective-permute-start | bytes 1032200 | tf_op jit(solution)/shard_map/ppermute | solution.py:165
  27.4 0.0 collective-permute-done.1.arrived_ref
  27.4 5.2 %collective-permute-done.3.last_ref = bf16[192,896]{1,0:T(8,128)(2,1)S(1)} collective-permute-done((bf16[192,896]{1,0:T(8,128)(2,1)S(1)}, bf16[192,896]{1,0:T(8,128)(2,1)S(1)}, u32[]{:S(2)}, u32[]{:S(2)}) %collective-permute-start.3) | collective-permute-done | bytes 344096 | tf_op jit(solution)/shard_map/ppermute | solution.py:165
  32.6 0.0 copy-start.1
  32.6 0.0 copy-start.2
  32.7 0.0 copy-start.3
  32.7 0.1 group_sums.1
  32.8 0.1 reshape.16
  32.9 35.2 %all_to_all.5 = bf16[96,2,1024]{2,1,0:T(2,128)(2,1)S(1)} all-to-all(bf16[96,2,1024]{2,1,0:T(2,128)(2,1)S(1)} %reshape.16), channel_id=1, replica_groups={{0,520,752,696,352,488,336,664,704,456,688,632,288,424,272,600,640,392,..., dimensions={0} | all-to-all | bytes 786432 | tf_op jit(solution)/shard_map/all_to_all | solution.py:190
  68.2 0.1 reshape.17.sums_ref
  68.3 0.0 copy-done.1
  68.3 0.0 copy-done.2
  68.4 0.0 copy-done.3
  68.4 1.7 %update.1 = (f32[192,896]{1,0:T(8,128)}, bf16[192,896]{1,0:T(8,128)(2,1)}, bf16[192,896]{1,0:T(8,128)(2,1)}) custom-call(bf16[192,1024]{1,0:T(8,128)(2,1)S(1)} %reshape.17.sums_ref, f32[192,896]{1,0:T(8,128)S(1)} %copy-done.1, bf16[192,896]{1,0:T(8,128)(2,1)S(1)} %copy-done.2, bf16[192,896]{1,0:T(8,128)(2,1)S(1)} %copy-done.3), custom_call_target="tpu_custom_call" | custom-call | tf_op jit(solution)/shard_map/update/pallas_call | solution.py:196
Async XLA Ops:
  0.6 5.9 %collective-permute-start = (bf16[128,7168]{1,0:T(8,128)(2,1)}, bf16[128,7168]{1,0:T(8,128)(2,1)S(1)}, u32[]{:S(2)}, u32[]{:S(2)}) collective-permute-start(bf16[128,7168]{1,0:T(8,128)(2,1)} %refs_2_.1), channel_id=1, source_target_pairs={{0,1},{1,0},{2,3},{3,2},{4,5},{5,4},{6,7},{7,6},{8,9},{9,8},{10,11... | collective-permute-start | bytes 5505032 | tf_op jit(solution)/shard_map/ppermute | solution.py:131
  2.6 1.5 %copy-start = (bf16[128,7168]{1,0:T(8,128)(2,1)S(1)}, bf16[128,7168]{1,0:T(8,128)(2,1)}, u32[]{:S(2)}) copy-start(bf16[128,7168]{1,0:T(8,128)(2,1)} %refs_2_.1) | copy-start | bytes 5505028
  4.1 0.7 copy-start.4
  4.7 0.7 copy-start.5
  6.8 9.1 %collective-permute-start.2 = (bf16[192,896]{1,0:T(8,128)(2,1)S(1)}, bf16[192,896]{1,0:T(8,128)(2,1)S(1)}, u32[]{:S(2)}, u32[]{:S(2)}) collective-permute-start(bf16[192,896]{1,0:T(8,128)(2,1)S(1)} %chip_sums.5), channel_id=1, source_target_pairs={{0,2},{1,7},{2,0},{3,5},{4,6},{5,3},{6,4},{7,1},{8,10},{9,15},{10,... | collective-permute-start | bytes 1032200 | tf_op jit(solution)/shard_map/ppermute | solution.py:165
  9.8 17.6 %collective-permute-start.1 = (bf16[192,896]{1,0:T(8,128)(2,1)S(1)}, bf16[192,896]{1,0:T(8,128)(2,1)S(1)}, u32[]{:S(2)}, u32[]{:S(2)}) collective-permute-start(bf16[192,896]{1,0:T(8,128)(2,1)S(1)} %chip_sums.4), channel_id=1, source_target_pairs={{0,2},{1,7},{2,0},{3,5},{4,6},{5,3},{6,4},{7,1},{8,10},{9,15},{10,... | collective-permute-start | bytes 1032200 | tf_op jit(solution)/shard_map/ppermute | solution.py:165
  16.0 16.6 %collective-permute-start.3 = (bf16[192,896]{1,0:T(8,128)(2,1)S(1)}, bf16[192,896]{1,0:T(8,128)(2,1)S(1)}, u32[]{:S(2)}, u32[]{:S(2)}) collective-permute-start(bf16[192,896]{1,0:T(8,128)(2,1)S(1)} %pair_sums.1), channel_id=1, source_target_pairs={{0,6},{1,3},{2,4},{3,1},{4,2},{5,7},{6,0},{7,5},{8,14},{9,11},{10,... | collective-permute-start | bytes 1032200 | tf_op jit(solution)/shard_map/ppermute | solution.py:165
  32.6 35.7 %copy-start.1 = (f32[192,896]{1,0:T(8,128)S(1)}, f32[192,896]{1,0:T(8,128)}, u32[]{:S(2)}) copy-start(f32[192,896]{1,0:T(8,128)} %param_ref.1) | copy-start | bytes 2064388
  32.6 35.7 %copy-start.2 = (bf16[192,896]{1,0:T(8,128)(2,1)S(1)}, bf16[192,896]{1,0:T(8,128)(2,1)}, u32[]{:S(2)}) copy-start(bf16[192,896]{1,0:T(8,128)(2,1)} %first_ref.1) | copy-start | bytes 1032196
  32.7 35.7 %copy-start.3 = (bf16[192,896]{1,0:T(8,128)(2,1)S(1)}, bf16[192,896]{1,0:T(8,128)(2,1)}, u32[]{:S(2)}) copy-start(bf16[192,896]{1,0:T(8,128)(2,1)} %second_ref.1) | copy-start | bytes 1032196

commit v6 on v5

--- a/solution.py
+++ b/solution.py
@@ -4,6 +4,7 @@
 from jax.experimental import pallas as pl
 from jax.experimental.pallas import tpu as pltpu
 from jax.sharding import Mesh, PartitionSpec as P
+import numpy as np
 
 BETA_ONE = 0.9
 BETA_TWO = 0.95
@@ -13,14 +14,13 @@
 CORRECT_ONE = 1.0 - 0.9**10
 CORRECT_TWO = 1.0 - 0.95**10
 CAP = 2
-SPREAD = (35, 30)
 LANES = 128
 VMEM = pl.BlockSpec(memory_space=pltpu.VMEM)
 HBM = pl.BlockSpec(memory_space=pltpu.HBM)
 
 
-def member(place, groups):
-    return place * (SPREAD[0] + SPREAD[1] * place) % groups
+def member_order(groups):
+    return np.random.RandomState(3).permutation(groups).tolist()
 
 
 def one_hot(mask):
@@ -54,16 +54,21 @@
         copy.start()
     for copy in small:
         copy.wait()
-    row = lax.broadcasted_iota(jnp.int32, (slots, LANES), 0)
-    owner = member(row // CAP, slots // CAP)
-    source = jnp.broadcast_to((CAP * owner + row % CAP)[:, :1], (slots, slots))
+    place = lax.broadcasted_iota(jnp.int32, (1, slots), 1) // CAP
+    owner_row = jnp.zeros((1, slots), jnp.int32)
+    for i, member in enumerate(member_order(slots // CAP)):
+        owner_row = jnp.where(place == i, member, owner_row)
+    row = lax.broadcasted_iota(jnp.int32, (slots, slots), 0)
     lane = lax.broadcasted_iota(jnp.int32, (slots, slots), 1)
+    wide = jnp.broadcast_to(owner_row, (slots, slots))
+    owner = jnp.sum(jnp.where(lane == row, wide, 0), axis=1, keepdims=True)
     wide = jnp.broadcast_to(slot_row[...], (slots, slots))
-    column = jnp.sum(jnp.where(lane == source, wide, 0), axis=1, keepdims=True)
+    column = jnp.sum(jnp.where(lane == CAP * owner + row % CAP, wide, 0), axis=1, keepdims=True)
     low, high = tokens[:, :half], tokens[:, half:]
     hot_ref[:, :half] = one_hot(column == jnp.where(c == 0, low, high))
     hot_ref[:, half:] = one_hot(column == jnp.where(c == 0, high, low))
     local = jnp.where(column < 0, -1, column - owner * block_rows)
+    local = jnp.broadcast_to(local, (slots, LANES))
     rows_ref[...] = local.astype(jnp.float32).astype(jnp.bfloat16)
     for copy in large:
         copy.wait()
@@ -186,7 +191,7 @@
     )(rows, kept, second, last)
     outgoing = outgoing.reshape(slots // CAP, CAP, cols + LANES)
     groups = slots // CAP
-    order = [member(place, groups) for place in range(groups)]
+    order = member_order(groups)
     slot_sums = lax.all_to_all(
         outgoing, "vocab", split_axis=0, concat_axis=0, axis_index_groups=[order], tiled=True
     )

time: 71 us -> 66.8 us (0.941)
  blocking collectives: 35.2 us -> 31.6 us
    all_to_all x1, blocking collectives: 35.2 us -> 31.6 us  [per_device(): lax.all_to_all(outgoing, 'vocab', split_axis=0, concat_axis=0, axis_index...]
where the time goes in v6:
time: 66.8 us; the launch traced here: 66.4 us
  blocking collectives  31.6 us (47%)
  starting transfers between devices  19.2 us (29%)
  waiting for transfers between devices  8.42 us (13%)
  Pallas kernels  3.36 us (5%)
  local copies, waits for them, and re-layouts  3.17 us (5%)
  between operations  0.76 us (1%)
    all_to_all x1, blocking collectives, per_device(): lax.all_to_all(outgoing, 'vocab', split_axis=0, concat_axis=0, axis_index...  31.6 us
    ppermute x3, starting transfers between devices, exchange(): return lax.ppermute(values, ('x', 'c'), list(enumerate(to)))  17.2 us
    ppermute x3, waiting for transfers between devices, exchange(): return lax.ppermute(values, ('x', 'c'), list(enumerate(to)))  7.81 us
    unnamed x12, local copies, waits for them, and re-layouts  2.87 us
    ppermute x1, starting transfers between devices, per_device(): other = lax.ppermute(grad_out, 'c', [(0, 1), (1, 0)])  1.92 us
    pallas_call x1, Pallas kernels, per_device(): pl.pallas_call(update_kernel, out_shape=(jax.ShapeDtypeStruct(param.shape...  1.74 us
  transfers between devices with their start and end apart: 4, of which 3 were waited for; matrix products, arithmetic and copies ran while one was open for 0% of the time, Pallas kernels for 2%

profile of v6, /device:TPU:6, one launch (start us, length us, event | category | flops | bytes accessed | tf_op | source)
XLA Modules:
  0.0 66.4 jit_solution(3515811468442942886)
XLA Ops:
  0.6 1.9 %collective-permute-start = (bf16[128,7168]{1,0:T(8,128)(2,1)}, bf16[128,7168]{1,0:T(8,128)(2,1)S(1)}, u32[]{:S(2)}, u32[]{:S(2)}) collective-permute-start(bf16[128,7168]{1,0:T(8,128)(2,1)} %refs_2_.1), channel_id=1, source_target_pairs={{0,1},{1,0},{2,3},{3,2},{4,5},{5,4},{6,7},{7,6},{8,9},{9,8},{10,11... | collective-permute-start | bytes 5505032 | tf_op jit(solution)/shard_map/ppermute | solution.py:136
  2.6 0.0 copy-start
  2.6 1.5 %copy-done = bf16[128,7168]{1,0:T(8,128)(2,1)S(1)} copy-done((bf16[128,7168]{1,0:T(8,128)(2,1)S(1)}, bf16[128,7168]{1,0:T(8,128)(2,1)}, u32[]{:S(2)}) %copy-start) | copy-done | bytes 1835032
  4.1 0.0 copy-start.4
  4.1 0.7 %copy-done.4 = s32[1024]{0:T(1024)S(1)} copy-done((s32[1024]{0:T(1024)S(1)}, s32[1024]{0:T(1024)}, u32[]{:S(2)}) %copy-start.4) | copy-done | bytes 4120
  4.7 0.0 copy-start.5
  4.7 0.7 %copy-done.5 = s32[1,192]{1,0:T(1,128)S(1)} copy-done((s32[1,192]{1,0:T(1,128)S(1)}, s32[1,192]{1,0:T(1,128)}, u32[]{:S(2)}) %copy-start.5) | copy-done | bytes 792
  5.4 0.5 setup.1
  5.9 0.6 collective-permute-done.refs_2_
  6.5 0.3 chip_sums.5
  6.8 2.7 %collective-permute-start.2 = (bf16[192,896]{1,0:T(8,128)(2,1)S(1)}, bf16[192,896]{1,0:T(8,128)(2,1)S(1)}, u32[]{:S(2)}, u32[]{:S(2)}) collective-permute-start(bf16[192,896]{1,0:T(8,128)(2,1)S(1)} %chip_sums.5), channel_id=1, source_target_pairs={{0,2},{1,7},{2,0},{3,5},{4,6},{5,3},{6,4},{7,1},{8,10},{9,15},{10,... | collective-permute-start | bytes 1032200 | tf_op jit(solution)/shard_map/ppermute | solution.py:170
  9.5 0.3 chip_sums.4
  9.8 3.1 %collective-permute-start.1 = (bf16[192,896]{1,0:T(8,128)(2,1)S(1)}, bf16[192,896]{1,0:T(8,128)(2,1)S(1)}, u32[]{:S(2)}, u32[]{:S(2)}) collective-permute-start(bf16[192,896]{1,0:T(8,128)(2,1)S(1)} %chip_sums.4), channel_id=1, source_target_pairs={{0,2},{1,7},{2,0},{3,5},{4,6},{5,3},{6,4},{7,1},{8,10},{9,15},{10,... | collective-permute-start | bytes 1032200 | tf_op jit(solution)/shard_map/ppermute | solution.py:170
  12.9 0.4 chip_sums.3
  13.3 2.6 %collective-permute-done.2.arrived_ref = bf16[192,896]{1,0:T(8,128)(2,1)S(1)} collective-permute-done((bf16[192,896]{1,0:T(8,128)(2,1)S(1)}, bf16[192,896]{1,0:T(8,128)(2,1)S(1)}, u32[]{:S(2)}, u32[]{:S(2)}) %collective-permute-start.2) | collective-permute-done | bytes 344096 | tf_op jit(solution)/shard_map/ppermute | solution.py:170
  15.9 0.1 pair_sums.1
  16.0 11.4 %collective-permute-start.3 = (bf16[192,896]{1,0:T(8,128)(2,1)S(1)}, bf16[192,896]{1,0:T(8,128)(2,1)S(1)}, u32[]{:S(2)}, u32[]{:S(2)}) collective-permute-start(bf16[192,896]{1,0:T(8,128)(2,1)S(1)} %pair_sums.1), channel_id=1, source_target_pairs={{0,6},{1,3},{2,4},{3,1},{4,2},{5,7},{6,0},{7,5},{8,14},{9,11},{10,... | collective-permute-start | bytes 1032200 | tf_op jit(solution)/shard_map/ppermute | solution.py:170
  27.4 0.0 collective-permute-done.1.arrived_ref
  27.4 5.2 %collective-permute-done.3.last_ref = bf16[192,896]{1,0:T(8,128)(2,1)S(1)} collective-permute-done((bf16[192,896]{1,0:T(8,128)(2,1)S(1)}, bf16[192,896]{1,0:T(8,128)(2,1)S(1)}, u32[]{:S(2)}, u32[]{:S(2)}) %collective-permute-start.3) | collective-permute-done | bytes 344096 | tf_op jit(solution)/shard_map/ppermute | solution.py:170
  32.6 0.0 copy-start.1
  32.6 0.0 copy-start.2
  32.7 0.0 copy-start.3
  32.7 0.1 group_sums.1
  32.8 0.1 reshape.16
  32.9 31.6 %all_to_all.5 = bf16[96,2,1024]{2,1,0:T(2,128)(2,1)S(1)} all-to-all(bf16[96,2,1024]{2,1,0:T(2,128)(2,1)S(1)} %reshape.16), channel_id=1, replica_groups={{488,184,752,72,200,48,632,568,456,512,120,616,464,560,648,360,624,712,..., dimensions={0} | all-to-all | bytes 786432 | tf_op jit(solution)/shard_map/all_to_all | solution.py:195
  64.5 0.1 reshape.17.sums_ref
  64.7 0.0 copy-done.1
  64.7 0.0 copy-done.2
  64.7 0.0 copy-done.3
  64.7 1.7 %update.1 = (f32[192,896]{1,0:T(8,128)}, bf16[192,896]{1,0:T(8,128)(2,1)}, bf16[192,896]{1,0:T(8,128)(2,1)}) custom-call(bf16[192,1024]{1,0:T(8,128)(2,1)S(1)} %reshape.17.sums_ref, f32[192,896]{1,0:T(8,128)S(1)} %copy-done.1, bf16[192,896]{1,0:T(8,128)(2,1)S(1)} %copy-done.2, bf16[192,896]{1,0:T(8,128)(2,1)S(1)} %copy-done.3), custom_call_target="tpu_custom_call" | custom-call | tf_op jit(solution)/shard_map/update/pallas_call | solution.py:201
Async XLA Ops:
  0.6 5.9 %collective-permute-start = (bf16[128,7168]{1,0:T(8,128)(2,1)}, bf16[128,7168]{1,0:T(8,128)(2,1)S(1)}, u32[]{:S(2)}, u32[]{:S(2)}) collective-permute-start(bf16[128,7168]{1,0:T(8,128)(2,1)} %refs_2_.1), channel_id=1, source_target_pairs={{0,1},{1,0},{2,3},{3,2},{4,5},{5,4},{6,7},{7,6},{8,9},{9,8},{10,11... | collective-permute-start | bytes 5505032 | tf_op jit(solution)/shard_map/ppermute | solution.py:136
  2.6 1.5 %copy-start = (bf16[128,7168]{1,0:T(8,128)(2,1)S(1)}, bf16[128,7168]{1,0:T(8,128)(2,1)}, u32[]{:S(2)}) copy-start(bf16[128,7168]{1,0:T(8,128)(2,1)} %refs_2_.1) | copy-start | bytes 5505028
  4.1 0.7 %copy-start.4 = (s32[1024]{0:T(1024)S(1)}, s32[1024]{0:T(1024)}, u32[]{:S(2)}) copy-start(s32[1024]{0:T(1024)} %param.7) | copy-start | bytes 12292
  4.7 0.7 %copy-start.5 = (s32[1,192]{1,0:T(1,128)S(1)}, s32[1,192]{1,0:T(1,128)}, u32[]{:S(2)}) copy-start(s32[1,192]{1,0:T(1,128)} %refs_1_.1) | copy-start | bytes 2308
  6.8 9.1 %collective-permute-start.2 = (bf16[192,896]{1,0:T(8,128)(2,1)S(1)}, bf16[192,896]{1,0:T(8,128)(2,1)S(1)}, u32[]{:S(2)}, u32[]{:S(2)}) collective-permute-start(bf16[192,896]{1,0:T(8,128)(2,1)S(1)} %chip_sums.5), channel_id=1, source_target_pairs={{0,2},{1,7},{2,0},{3,5},{4,6},{5,3},{6,4},{7,1},{8,10},{9,15},{10,... | collective-permute-start | bytes 1032200 | tf_op jit(solution)/shard_map/ppermute | solution.py:170
  9.8 17.6 %collective-permute-start.1 = (bf16[192,896]{1,0:T(8,128)(2,1)S(1)}, bf16[192,896]{1,0:T(8,128)(2,1)S(1)}, u32[]{:S(2)}, u32[]{:S(2)}) collective-permute-start(bf16[192,896]{1,0:T(8,128)(2,1)S(1)} %chip_sums.4), channel_id=1, source_target_pairs={{0,2},{1,7},{2,0},{3,5},{4,6},{5,3},{6,4},{7,1},{8,10},{9,15},{10,... | collective-permute-start | bytes 1032200 | tf_op jit(solution)/shard_map/ppermute | solution.py:170
  16.0 16.6 %collective-permute-start.3 = (bf16[192,896]{1,0:T(8,128)(2,1)S(1)}, bf16[192,896]{1,0:T(8,128)(2,1)S(1)}, u32[]{:S(2)}, u32[]{:S(2)}) collective-permute-start(bf16[192,896]{1,0:T(8,128)(2,1)S(1)} %pair_sums.1), channel_id=1, source_target_pairs={{0,6},{1,3},{2,4},{3,1},{4,2},{5,7},{6,0},{7,5},{8,14},{9,11},{10,... | collective-permute-start | bytes 1032200 | tf_op jit(solution)/shard_map/ppermute | solution.py:170
  32.6 32.0 %copy-start.1 = (f32[192,896]{1,0:T(8,128)S(1)}, f32[192,896]{1,0:T(8,128)}, u32[]{:S(2)}) copy-start(f32[192,896]{1,0:T(8,128)} %param_ref.1) | copy-start | bytes 2064388
  32.6 32.0 %copy-start.2 = (bf16[192,896]{1,0:T(8,128)(2,1)S(1)}, bf16[192,896]{1,0:T(8,128)(2,1)}, u32[]{:S(2)}) copy-start(bf16[192,896]{1,0:T(8,128)(2,1)} %first_ref.1) | copy-start | bytes 1032196
  32.7 32.0 %copy-start.3 = (bf16[192,896]{1,0:T(8,128)(2,1)S(1)}, bf16[192,896]{1,0:T(8,128)(2,1)}, u32[]{:S(2)}) copy-start(bf16[192,896]{1,0:T(8,128)(2,1)} %second_ref.1) | copy-start | bytes 1032196
